TPU v7x, 128 devices: a whole 4x4x4 slice. The times are simulated.
128 devices in a mesh: tok: 16 (over y, x), exp: 8 (over z, core).
Axes of the slice: x: 4, y: 4, z: 4, core: 2. Of those that a mesh axis runs over, the one named last changes fastest.
Arguments:
- tokens: bfloat16 [16384, 2560], P('exp', 'tok'), may hold values from -6 to 6
- grad_out: bfloat16 [16384, 2560], P('exp', 'tok'), may hold values from -6 to 6
- gate_probs: float32 [16384, 6], P('exp'), may hold values from 0.05 to 0.5
- routes: int32 [16384, 6], P('exp'), may hold values from 0 to 15, all different within a row; in each aligned block of 2048 rows (0 to 2047, 2048 to 4095, ...) at most 1536 rows name the same one
- need_lists: int32 [8, 16], replicated, may hold values from 0 to 79, as said below
- up_weight: bfloat16 [80, 2560, 768], P('exp', 'tok'), may hold values from -0.125 to 0.125
- down_weight: bfloat16 [80, 2560, 768], P('exp', 'tok'), may hold values from -0.21875 to 0.21875
Outputs:
- token_grads: bfloat16 [16384, 2560], P('exp', 'tok')
- gate_grads: float32 [16384, 6], P('exp')
- up_grads: bfloat16 [80, 2560, 768], P('exp', 'tok')
- down_grads: bfloat16 [80, 2560, 768], P('exp', 'tok')
Inputs may be any that keep to these rules, and one draw needn't show every extreme that they name: `routes`: within each aligned block of 2048 rows (one index of exp) a row names 6 different slots; no slot is named by more than 1536 rows of a block, and in every draw some slot is named by exactly 1536 rows of some block. `need_lists`: each row holds 16 different experts; entries 2 * o to 2 * o + 1 of a row lie in o * 10 to o * 10 + 9, the experts of exp index o.
All inputs are finite; a program needn't handle non-finite values.
Results may differ from a plain program's by a relative error of at most 0.007.
Values may be sent and summed in bfloat16 or wider, within the bound.
A program may use at most 384 MiB of HBM per device.

v0:
```python
import jax
import jax.numpy as jnp
from jax import lax
from jax.sharding import PartitionSpec as P

TOPK = 6


def silu_parts(pre_act):
    sigmoid_value = jax.nn.sigmoid(pre_act)
    return (pre_act * sigmoid_value, sigmoid_value * (1.0 + pre_act * (1.0 - sigmoid_value)))


def hidden_step(pre_act, hidden_grad, slot_prob):
    activated, silu_slope = silu_parts(pre_act)
    activation = activated.astype(jnp.bfloat16)
    prob_grad = jnp.sum(activation.astype(jnp.float32) * hidden_grad, axis=1)
    pre_grad = (slot_prob[:, None] * hidden_grad * silu_slope).astype(jnp.bfloat16)
    return (activation, pre_grad, prob_grad)


def slot_tables(routes, gate_probs, n_slots, capacity):
    rows_col = routes.shape[0]
    slot_ids = jnp.arange(n_slots, dtype=jnp.int32)
    slot_hits = routes[None, :, :] == slot_ids[:, None, None]
    member = jnp.any(slot_hits, axis=2)
    prob_rows = jnp.sum(jnp.where(slot_hits, gate_probs[None, :, :], 0.0), axis=2)
    position = jnp.cumsum(member.astype(jnp.int32), axis=1) - 1
    cap_ids = jnp.arange(capacity, dtype=jnp.int32)
    matched = (position[:, None, :] == cap_ids[None, :, None]) & member[:, None, :]
    row_ids = jnp.arange(rows_col, dtype=jnp.int32)
    indices = jnp.sum(jnp.where(matched, row_ids[None, None, :], 0), axis=2)
    filled = jnp.any(matched, axis=2)
    slot_probs = jnp.sum(jnp.where(matched, prob_rows[:, None, :], 0.0), axis=2)
    return (indices, filled, slot_probs)


def body(tokens, grad_out, gate_probs, routes, need_lists, up_weight, down_weight):
    tok_count = lax.axis_size("tok")
    exp_count = lax.axis_size("exp")
    tok_index = lax.axis_index("tok")
    exp_index = lax.axis_index("exp")
    per_owner = tok_count // exp_count
    experts_here = up_weight.shape[0]
    rows_col = routes.shape[0]
    capacity = min(rows_col, 2 * rows_col * TOPK // tok_count)
    zero_value = jnp.zeros((), jnp.bfloat16)
    need_grid = need_lists.reshape(exp_count, exp_count, per_owner)
    local_ids = (jnp.take(need_grid, exp_index, axis=1) - exp_index * experts_here).reshape(-1)
    owned_hot = (local_ids[None, :] == jnp.arange(experts_here, dtype=jnp.int32)[:, None]).astype(
        jnp.bfloat16
    )
    send_up = jnp.take(up_weight, local_ids, axis=0)
    send_down = jnp.take(down_weight, local_ids, axis=0)
    indices, filled, slot_probs = slot_tables(routes, gate_probs, tok_count, capacity)
    own_rows = jnp.take(indices, tok_index, axis=0)
    own_filled = jnp.take(filled, tok_index, axis=0)
    own_probs = jnp.take(slot_probs, tok_index, axis=0)
    fetched_up, fetched_down = (
        lax.all_to_all(
            lax.all_to_all(send_up, "exp", split_axis=0, concat_axis=0, tiled=True),
            "tok",
            split_axis=0,
            concat_axis=1,
            tiled=True,
        ),
        lax.all_to_all(
            lax.all_to_all(send_down, "exp", split_axis=0, concat_axis=0, tiled=True),
            "tok",
            split_axis=0,
            concat_axis=1,
            tiled=True,
        ),
    )
    up_matrix = fetched_up[0]
    down_matrix = fetched_down[0]
    full_tokens, full_grads = (
        lax.all_gather(tokens, "tok", axis=1, tiled=True),
        lax.all_gather(grad_out, "tok", axis=1, tiled=True),
    )
    token_rows = jnp.where(own_filled[:, None], jnp.take(full_tokens, own_rows, axis=0), zero_value)
    grad_rows = jnp.where(own_filled[:, None], jnp.take(full_grads, own_rows, axis=0), zero_value)
    pre_act = jnp.dot(token_rows, up_matrix, preferred_element_type=jnp.float32)
    hidden_grad = jnp.dot(grad_rows, down_matrix, preferred_element_type=jnp.float32)
    activation, pre_grad, prob_grad = hidden_step(pre_act, hidden_grad, own_probs)
    scaled = (own_probs[:, None] * grad_rows.astype(jnp.float32)).astype(jnp.bfloat16)
    input_part = lax.dot_general(
        pre_grad, up_matrix, (((1,), (1,)), ((), ())), preferred_element_type=jnp.float32
    )
    input_part = jnp.where(own_filled[:, None], input_part, 0.0)
    grad_up = lax.dot_general(
        token_rows, pre_grad, (((0,), (0,)), ((), ())), preferred_element_type=jnp.float32
    ).astype(jnp.bfloat16)
    grad_down = lax.dot_general(
        scaled, activation, (((0,), (0,)), ((), ())), preferred_element_type=jnp.float32
    ).astype(jnp.bfloat16)
    spread = jnp.zeros((rows_col, full_tokens.shape[1]), jnp.float32).at[own_rows].add(input_part)
    token_grads = lax.psum_scatter(spread, "tok", scatter_dimension=1, tiled=True).astype(
        jnp.bfloat16
    )
    returned_up, returned_down = (
        lax.all_to_all(
            lax.all_to_all(grad_up[None], "tok", split_axis=1, concat_axis=0, tiled=True),
            "exp",
            split_axis=0,
            concat_axis=0,
            tiled=True,
        ),
        lax.all_to_all(
            lax.all_to_all(grad_down[None], "tok", split_axis=1, concat_axis=0, tiled=True),
            "exp",
            split_axis=0,
            concat_axis=0,
            tiled=True,
        ),
    )
    token_prob = (
        jnp.zeros((rows_col,), jnp.float32).at[own_rows].add(jnp.where(own_filled, prob_grad, 0.0))
    )
    gate_grads = lax.psum(jnp.where(routes == tok_index, token_prob[:, None], 0.0), "tok")
    up_grads = jnp.einsum(
        "en,ndh->edh", owned_hot, returned_up, preferred_element_type=jnp.float32
    ).astype(jnp.bfloat16)
    down_grads = jnp.einsum(
        "en,ndh->edh", owned_hot, returned_down, preferred_element_type=jnp.float32
    ).astype(jnp.bfloat16)
    return (token_grads, gate_grads, up_grads, down_grads)


def solution(mesh):
    placed = (
        P("exp", "tok"),
        P("exp", "tok"),
        P("exp", None),
        P("exp", None),
        P(),
        P("exp", "tok", None),
        P("exp", "tok", None),
    )
    return jax.shard_map(
        body,
        mesh=mesh,
        in_specs=placed,
        out_specs=(P("exp", "tok"), P("exp", None), P("exp", "tok", None), P("exp", "tok", None)),
        check_vma=False,
    )
```

profile of v0, /device:TPU:0, one launch (start us, length us, event | category | flops | bytes accessed | tf_op | source)
XLA Modules:
  0.0 890.6 jit_solution(11677034665279411253)
XLA Ops:
  7.2 0.0 all-gather.5.cloned.1.call-start
  7.2 0.7 all-gather.5.cloned.1.call-update
  7.9 0.8 copy.59
  8.7 0.1 copy.60
  8.8 0.1 sub.27
  8.9 2.7 gather_fusion.3
  11.5 4.4 gather_fusion.1
  16.0 7.2 broadcast_select_fusion.1
  23.2 5.6 all-to-all-start
  28.8 0.0 all-gather.3.cloned.1.call-start
  28.9 0.7 all-gather.3.cloned.1.call-update
  29.6 0.1 fusion.22
  29.8 4.5 reduce-window.6
  34.3 0.4 slice_reduce_fusion
  34.7 0.2 reduce-window.9
  34.9 0.1 add_add_fusion
  35.1 0.1 select_reduce_fusion.2
  35.2 40.6 %all-to-all-done = bf16[16,160,768]{2,1,0:T(8,128)(2,1)} async-done(((bf16[16,160,768]{2,1,0:T(8,128)(2,1)}), bf16[16,160,768]{2,1,0:T(8,128)(2,1)}, u32[]{:S(2)}, u32[]{:S(2)}) %all-to-all-start) | async-done | bytes 3932192 | tf_op jit(solution)/shard_map/all_to_all | solution.py:68
  75.8 4.6 all-to-all-start.2
  80.4 43.7 %select_reduce_fusion = f32[16,1536]{1,0:T(8,128)S(1)} fusion(f32[16,2048]{1,0:T(8,128)S(1)} %select_reduce_fusion.2, s32[16,2048]{1,0:T(8,128)S(1)} %bitcast.50, pred[16,2048]{1,0:T(8,128)(4,1)S(1)} %fusion.22), kind=kLoop, calls=%fused_computation.6 | loop fusion | flops 201302016 | bytes 393216 | tf_op jit(solution)/shard_map/reduce_sum | solution.py:34
  124.1 3.1 all-to-all-done.2
  127.2 7.1 all-to-all-start.3
  134.3 43.8 %select_reduce_fusion.1 = s32[16,1536]{1,0:T(8,128)S(1)} fusion(s32[16,2048]{1,0:T(8,128)S(1)} %bitcast.51, pred[16,2048]{1,0:T(8,128)(4,1)S(1)} %fusion.22), kind=kLoop, calls=%fused_computation.7 | loop fusion | flops 201302016 | bytes 262144 | tf_op jit(solution)/shard_map/reduce_sum | solution.py:32
  178.1 42.3 %all-to-all-done.3 = bf16[16,160,768]{2,1,0:T(8,128)(2,1)} async-done(((bf16[16,160,768]{2,1,0:T(8,128)(2,1)}), bf16[16,160,768]{2,1,0:T(8,128)(2,1)}, u32[]{:S(2)}, u32[]{:S(2)}) %all-to-all-start.3) | async-done | bytes 3932192 | tf_op jit(solution)/shard_map/all_to_all | solution.py:60
  220.5 4.5 all-to-all-start.1
  225.0 0.6 reduce-scatter.4.cloned.1.call-start
  225.6 30.8 %fusion.1 = pred[16,1536]{1,0:T(8,128)(4,1)S(1)} fusion(s32[16,2048]{1,0:T(8,128)S(1)} %bitcast.52, pred[16,2048]{1,0:T(8,128)(4,1)S(1)} %fusion.22), kind=kLoop, calls=%fused_computation.10 | loop fusion | flops 150970368 | bytes 188416 | tf_op jit(solution)/shard_map/reduce_or | solution.py:33
  256.6 0.0 all-gather.5.cloned.1.call-done
  256.6 13.7 %copy.61 = bf16[2048,2560]{1,0:T(8,128)(2,1)} copy(bf16[2048,2560]{0,1:T(8,128)(2,1)} %all-gather.5.cloned.1.call-done) | data formatting | bytes 20971520 | tf_op jit(solution)/shard_map/all_gather | solution.py:78
  270.3 20.4 %gather_fusion.2 = bf16[1536,2560]{1,0:T(8,128)(2,1)} fusion(bf16[2048,2560]{1,0:T(8,128)(2,1)} %copy.61, s32[2048]{0:T(1024)S(1)} %pad_clamp_fusion), kind=kCustom, calls=%fused_computation.2.clone | custom fusion | bytes 15734784 | tf_op jit(solution)/shard_map/jit(_take)/gather | solution.py:81
  290.8 13.8 %copy.58 = bf16[2048,2560]{1,0:T(8,128)(2,1)} copy(bf16[2048,2560]{0,1:T(8,128)(2,1)} %all-gather.3.cloned.1.call-done) | data formatting | bytes 20971520 | tf_op jit(solution)/shard_map/all_gather | solution.py:79
  304.6 20.4 %gather_fusion = bf16[1536,2560]{1,0:T(8,128)(2,1)} fusion(bf16[2048,2560]{1,0:T(8,128)(2,1)} %copy.58, s32[2048]{0:T(1024)S(1)} %pad_clamp_fusion), kind=kCustom, calls=%fused_computation.clone | custom fusion | bytes 15734784 | tf_op jit(solution)/shard_map/jit(_take)/gather | solution.py:82
  325.0 12.4 %fusion.34 = f32[1536,768]{0,1:T(8,128)} fusion(bf16[2560,768]{1,0:T(8,128)(2,1)} %bitcast.3, bf16[1536,2560]{1,0:T(8,128)(2,1)} %gather_fusion.2, pred[1536]{0:T(1024)(128)(4,1)S(1)} %compare_and_fusion, pred[1536]{0:T(1024)(128)(4,1)S(1)} %select_reduce_fusion.3), kind=kOutput, calls=%fused_computation.67 | convolution fusion | flops 6047662080 | bytes 16518144 | tf_op jit(solution)/shard_map/dot_general | solution.py:83
  337.4 13.2 %multiply_reduce_fusion = (f32[1536]{0:T(1024)S(1)}, bf16[1536,768]{0,1:T(8,128)(2,1)S(1)}) fusion(f32[1536,768]{0,1:T(8,128)} %fusion.34, f32[1536]{0:T(1024)S(1)} %fusion.27, bf16[2560,768]{1,0:T(8,128)(2,1)} %bitcast.2, bf16[1536,2560]{1,0:T(8,128)(2,1)} %gather_fusion, pred[1536]{0:T(1024)(128)(4,1)S(1)} %compare_and_fusion, ...), kind=kOutput, calls=%fused_computation.23 | convolution fusion | flops 6065355264 | bytes 18889728 | tf_op jit(solution)/shard_map/dot_general | solution.py:84
  350.7 11.5 %fusion.35 = f32[1536,2560]{1,0:T(8,128)} fusion(bf16[1536,768]{0,1:T(8,128)(2,1)S(1)} %get-tuple-element.71, bf16[2560,768]{1,0:T(8,128)(2,1)} %bitcast.3), kind=kOutput, calls=%fused_computation.70 | convolution fusion | flops 6039797760 | bytes 22020096 | tf_op jit(solution)/shard_map/dot_general | solution.py:87
  362.2 34.2 %scatter_custom_fusion = f32[2048,2560]{1,0:T(8,128)} fusion(s32[1536]{0:T(1024)S(1)} %fusion.26, f32[1536,2560]{1,0:T(8,128)} %fusion.35, f32[]{:T(128)} %constant.57.clone.1, pred[1536]{0:T(1024)(128)(4,1)S(1)} %select_reduce_fusion.3), kind=kCustom, calls=%fused_computation.12 | custom fusion | flops 7864320 | bytes 36703232 | tf_op jit(solution)/shard_map/scatter-add | solution.py:97
  396.4 21.6 %copy.69 = f32[2048,2560]{0,1:T(8,128)} copy(f32[2048,2560]{1,0:T(8,128)} %scatter_custom_fusion) | data formatting | bytes 41943040
  418.0 10.7 %fusion.10 = bf16[1,2560,768]{2,1,0:T(8,128)(2,1)S(1)} fusion(bf16[1536,768]{0,1:T(8,128)(2,1)S(1)} %get-tuple-element.71, bf16[1536,2560]{1,0:T(8,128)(2,1)} %gather_fusion.2, pred[1536]{0:T(1024)(128)(4,1)S(1)} %compare_and_fusion, pred[1536]{0:T(1024)(128)(4,1)S(1)} %select_reduce_fusion.3), kind=kOutput, calls=%fused_computation.27 | convolution fusion | flops 6049628160 | bytes 14158848 | tf_op jit(solution)/shard_map/dot_general | solution.py:91
  428.7 56.0 %copy.88 = bf16[1,2560,768]{2,0,1:T(2,128)(2,1)} copy(bf16[1,2560,768]{2,1,0:T(8,128)(2,1)S(1)} %fusion.10) | data formatting | bytes 7864320 | tf_op jit(solution)/shard_map/broadcast_in_dim | solution.py:103
  484.7 0.5 broadcast.258
  485.2 41.2 %reduce.10 = bf16[2560,768]{1,0:T(8,128)(2,1)} reduce(bf16[2560,1,768]{2,1,0:T(2,128)(2,1)} %bitcast.41, bf16[]{:T(256)} %broadcast.258), dimensions={1}, to_apply=%bitcast.38.reduce_sub_computation | reduce | bytes 7864322
  526.4 10.4 %reshape.297 = bf16[16,2,61440]{2,1,0:T(2,128)(2,1)} reshape(bf16[2560,768]{1,0:T(8,128)(2,1)} %reduce.10) | data formatting | bytes 7864320
  536.8 7.1 all-to-all-start.4
  544.0 13.9 %fusion.11 = bf16[1,2560,768]{2,1,0:T(8,128)(2,1)S(1)} fusion(f32[1536]{0:T(1024)S(1)} %fusion.27, bf16[1536,2560]{1,0:T(8,128)(2,1)} %gather_fusion, pred[1536]{0:T(1024)(128)(4,1)S(1)} %compare_and_fusion, pred[1536]{0:T(1024)(128)(4,1)S(1)} %select_reduce_fusion.3, f32[1536,768]{0,1:T(8,128)} %fusion.34), kind=kOutput, calls=%fused_computation.28 | convolution fusion | flops 6067322880 | bytes 16524288 | tf_op jit(solution)/shard_map/dot_general | solution.py:94
  557.8 56.1 %copy.87 = bf16[1,2560,768]{2,0,1:T(2,128)(2,1)} copy(bf16[1,2560,768]{2,1,0:T(8,128)(2,1)S(1)} %fusion.11) | data formatting | bytes 7864320 | tf_op jit(solution)/shard_map/broadcast_in_dim | solution.py:110
  613.9 41.2 %reduce.11 = bf16[2560,768]{1,0:T(8,128)(2,1)} reduce(bf16[2560,1,768]{2,1,0:T(2,128)(2,1)} %bitcast.42, bf16[]{:T(256)} %broadcast.258), dimensions={1}, to_apply=%bitcast.37.reduce_sub_computation | reduce | bytes 7864322
  655.1 10.4 %reshape.299 = bf16[16,2,61440]{2,1,0:T(2,128)(2,1)} reshape(bf16[2560,768]{1,0:T(8,128)(2,1)} %reduce.11) | data formatting | bytes 7864320
  665.6 7.2 all-to-all-start.6
  672.8 12.2 %reshape.298 = bf16[2560,1,768]{2,1,0:T(2,128)(2,1)} reshape(bf16[16,2,61440]{2,1,0:T(2,128)(2,1)} %all-to-all-done.4) | data formatting | bytes 7864320
  685.0 5.8 copy.71
  690.8 38.0 %all-to-all-done.6 = bf16[16,2,61440]{2,1,0:T(2,128)(2,1)} async-done(((bf16[16,2,61440]{2,1,0:T(2,128)(2,1)}), bf16[16,2,61440]{2,1,0:T(2,128)(2,1)}, u32[]{:S(2)}, u32[]{:S(2)}) %all-to-all-start.6) | async-done | bytes 3932192 | tf_op jit(solution)/shard_map/all_to_all | solution.py:110
  728.8 4.5 all-to-all-start.5
  733.3 12.2 %reshape.300 = bf16[2560,1,768]{2,1,0:T(2,128)(2,1)} reshape(bf16[16,2,61440]{2,1,0:T(2,128)(2,1)} %all-to-all-done.6) | data formatting | bytes 7864320
  745.5 5.8 copy.72
  751.3 28.8 %all-to-all-done.5 = bf16[16,160,768]{2,1,0:T(8,128)(2,1)} async-done(((bf16[16,160,768]{2,1,0:T(8,128)(2,1)}), bf16[16,160,768]{2,1,0:T(8,128)(2,1)}, u32[]{:S(2)}, u32[]{:S(2)}) %all-to-all-start.5) | async-done | bytes 3932192 | tf_op jit(solution)/shard_map/all_to_all | solution.py:102
  780.2 4.6 all-to-all-start.7
  784.7 11.1 %scatter_custom_fusion.1 = f32[2048]{0:T(1024)S(1)} fusion(s32[1536]{0:T(1024)S(1)} %fusion.26, f32[1536]{0:T(1024)S(1)} %broadcast_select_fusion.4, f32[]{:T(128)} %constant.57.clone.1), kind=kCustom, calls=%fused_computation.60 | custom fusion | flops 1536 | bytes 8196 | tf_op jit(solution)/shard_map/scatter-add | solution.py:118
  795.9 71.1 %psum.7 = f32[2048,6]{0,1:T(8,128)} all-reduce(f32[2048,6]{0,1:T(8,128)S(1)} %compare_select_fusion), channel_id=1, replica_groups=mesh['tok'=16,'exp'=8] {'tok'}, use_global_device_ids=true, to_apply=%region_11.14 | all-reduce | flops 12288 | bytes 98304 | tf_op jit(solution)/shard_map/psum | solution.py:120
  867.1 4.6 fusion.16
  871.7 2.2 copy.67
  873.9 4.7 fusion.19
  878.6 2.2 copy.68
  880.9 1.5 copy.70
  882.4 1.2 copy.66
  (36 shorter events, 0.3 us)
Async XLA Ops:
  7.2 1.7 copy-start
  7.2 249.4 %all-gather.5.cloned.1.call-start = ((), (), s32[]{:S(2)}) async-start(), calls=%async_computation.10 | async-start | bytes 11141120 | tf_op jit(solution)/shard_map/all_gather | solution.py:78
  8.9 7.1 copy-start.5
  23.2 6.3 copy-start.2
  23.2 11.8 %copy-start.4 = (f32[2048,6]{0,1:T(8,128)S(1)}, f32[2048,6]{0,1:T(8,128)}, u32[]{:S(2)}) copy-start(f32[2048,6]{0,1:T(8,128)} %param.13) | copy-start | bytes 147460
  23.2 52.6 %all-to-all-start = ((bf16[16,160,768]{2,1,0:T(8,128)(2,1)}), bf16[16,160,768]{2,1,0:T(8,128)(2,1)}, u32[]{:S(2)}, u32[]{:S(2)}) async-start(bf16[16,160,768]{2,1,0:T(8,128)(2,1)} %get-tuple-element.72), calls=%async_computation | async-start | bytes 7864320 | tf_op jit(solution)/shard_map/all_to_all | solution.py:68
  28.8 261.9 %all-gather.3.cloned.1.call-start = ((), (), s32[]{:S(2)}) async-start(), calls=%async_computation.9 | async-start | bytes 11141120 | tf_op jit(solution)/shard_map/all_gather | solution.py:79
  75.8 51.4 %all-to-all-start.2 = ((bf16[16,160,768]{2,1,0:T(8,128)(2,1)}), bf16[16,160,768]{2,1,0:T(8,128)(2,1)}, u32[]{:S(2)}, u32[]{:S(2)}) async-start(bf16[16,160,768]{2,1,0:T(8,128)(2,1)} %get-tuple-element.73), calls=%async_computation.2 | async-start | bytes 7864320 | tf_op jit(solution)/shard_map/all_to_all | solution.py:61
  127.2 93.2 %all-to-all-start.3 = ((bf16[16,160,768]{2,1,0:T(8,128)(2,1)}), bf16[16,160,768]{2,1,0:T(8,128)(2,1)}, u32[]{:S(2)}, u32[]{:S(2)}) async-start(bf16[16,160,768]{2,1,0:T(8,128)(2,1)} %all-to-all-done.2), calls=%async_computation.3 | async-start | bytes 7864320 | tf_op jit(solution)/shard_map/all_to_all | solution.py:60
  220.5 117.0 %all-to-all-start.1 = ((bf16[16,160,768]{2,1,0:T(8,128)(2,1)}), bf16[16,160,768]{2,1,0:T(8,128)(2,1)}, u32[]{:S(2)}, u32[]{:S(2)}) async-start(bf16[16,160,768]{2,1,0:T(8,128)(2,1)} %all-to-all-done), calls=%async_computation.1 | async-start | bytes 7864320 | tf_op jit(solution)/shard_map/all_to_all | solution.py:67
  225.0 655.9 %reduce-scatter.4.cloned.1.call-start = ((), (), s32[]{:S(2)}) async-start(), calls=%async_computation.11 | async-start | bytes 22282240
  536.8 128.7 %all-to-all-start.4 = ((bf16[16,2,61440]{2,1,0:T(2,128)(2,1)}), bf16[16,2,61440]{2,1,0:T(2,128)(2,1)}, u32[]{:S(2)}, u32[]{:S(2)}) async-start(bf16[16,2,61440]{2,1,0:T(2,128)(2,1)} %reshape.297), calls=%async_computation.4 | async-start | bytes 7864320 | tf_op jit(solution)/shard_map/all_to_all | solution.py:103
  665.6 63.2 %all-to-all-start.6 = ((bf16[16,2,61440]{2,1,0:T(2,128)(2,1)}), bf16[16,2,61440]{2,1,0:T(2,128)(2,1)}, u32[]{:S(2)}, u32[]{:S(2)}) async-start(bf16[16,2,61440]{2,1,0:T(2,128)(2,1)} %reshape.299), calls=%async_computation.6 | async-start | bytes 7864320 | tf_op jit(solution)/shard_map/all_to_all | solution.py:110
  728.8 51.4 %all-to-all-start.5 = ((bf16[16,160,768]{2,1,0:T(8,128)(2,1)}), bf16[16,160,768]{2,1,0:T(8,128)(2,1)}, u32[]{:S(2)}, u32[]{:S(2)}) async-start(bf16[16,160,768]{2,1,0:T(8,128)(2,1)} %bitcast.46), calls=%async_computation.5 | async-start | bytes 7864320 | tf_op jit(solution)/shard_map/all_to_all | solution.py:102
  751.3 44.6 %copy-start.3 = (s32[2048,6]{0,1:T(8,128)S(1)}, s32[2048,6]{0,1:T(8,128)}, u32[]{:S(2)}) copy-start(s32[2048,6]{0,1:T(8,128)} %param.14) | copy-start | bytes 147460
  751.3 115.7 %copy-start.6 = (s32[16]{0:T(128)S(1)}, s32[16]{0:T(128)}, u32[]{:S(2)}) copy-start(s32[16]{0:T(128)} %copy-done.5) | copy-start | bytes 196
  780.2 93.7 %all-to-all-start.7 = ((bf16[16,160,768]{2,1,0:T(8,128)(2,1)}), bf16[16,160,768]{2,1,0:T(8,128)(2,1)}, u32[]{:S(2)}, u32[]{:S(2)}) async-start(bf16[16,160,768]{2,1,0:T(8,128)(2,1)} %bitcast.45), calls=%async_computation.7 | async-start | bytes 7864320 | tf_op jit(solution)/shard_map/all_to_all | solution.py:109
  873.9 9.7 %copy-start.1 = (bf16[10,160,768]{2,1,0:T(8,128)(2,1)S(1)}, bf16[10,160,768]{2,1,0:T(8,128)(2,1)}, u32[]{:S(2)}) copy-start(bf16[10,160,768]{2,1,0:T(8,128)(2,1)} %param.16) | copy-start | bytes 7372804
Sparse Core Ops, SparseCore 0:
  10.2 82.7 all-gather.4
  95.1 122.0 all-gather.2
  418.2 149.4 reduce-scatter.3
where the time goes:
time: 898 us; the launch traced here: 891 us
  local copies, waits for them, and re-layouts  275 us (31%)
  other arithmetic  259 us (29%)
  waiting for transfers between devices  154 us (17%)
  blocking collectives  71.1 us (8%)
  matrix products  71 us (8%)
  starting transfers between devices  45.8 us (5%)
  between operations  14.5 us (2%)
    unnamed x29, local copies, waits for them, and re-layouts  87.1 us
    unnamed x3, other arithmetic  82.4 us
    psum x1, blocking collectives, body(): lax.psum(jnp.where(routes == tok_index, token_prob[:, None], 0.0), 'tok')  71.1 us
    broadcast_in_dim x1, local copies, waits for them, and re-layouts, body(): grad_down[None]  56.1 us
    broadcast_in_dim x1, local copies, waits for them, and re-layouts, body(): grad_up[None]  56 us
    reduce_sum x1, other arithmetic, slot_tables(): indices = jnp.sum(jnp.where(matched, row_ids[None, None, :], 0), axis=2)  43.8 us
    reduce_sum x1, other arithmetic, slot_tables(): slot_probs = jnp.sum(jnp.where(matched, prob_rows[:, None, :], 0.0), axis=2)  43.7 us
    all_to_all x1, waiting for transfers between devices, body(): lax.all_to_all(lax.all_to_all(send_up, 'exp', split_axis=0, concat_axis=0...  42.3 us
  transfers between devices with their start and end apart: 11, of which 5 were waited for; matrix products, arithmetic and copies ran while one was open for 59% of the time, Pallas kernels for 0%

commit v1 on v0

v1 whole, which is shorter than its diff:
```python
import functools

import jax
import jax.numpy as jnp
from jax import lax
from jax.experimental import pallas as pl
from jax.experimental.pallas import tpu as pltpu
from jax.sharding import PartitionSpec as P

MESH = pl.DeviceIdType.MESH
F32 = jnp.float32
BF16 = jnp.bfloat16


def loop(count, step):
    def run(i, carry):
        step(i)
        return carry

    lax.fori_loop(0, count, run, 0)


def layer_kernel(
    nt, ne, rows_dev, hid, cols, htile, ntile,
    sw, xs, p2,
    relay1, relay2, wout, trecv, gpart,
    xg, ww, pa, dw, cbuf, wt, pr, grow,
    s1, r1, st, tr, s2, wr, sf, ps, prs, sd, r2, sg, gr, cs, cr, ts, trr, fs, fr,
):
    t = lax.axis_index("tok")
    e = lax.axis_index("exp")
    z, k = lax.div(e, 2), lax.rem(e, 2)
    q, h = lax.div(t, 2), lax.rem(t, 2)
    nz = ne // 2
    sibling = 2 * z + 1 - k
    column_core = 2 * z + h

    def remote(src, dst, send, recv, tok, ex):
        return pltpu.make_async_remote_copy(
            src_ref=src, dst_ref=dst, send_sem=send, recv_sem=recv,
            device_id=(tok, ex), device_id_type=MESH,
        )

    def push(src, dst, send, recv, tok, ex):
        own = jnp.logical_and(tok == t, ex == e)

        @pl.when(own)
        def _():
            pltpu.make_async_copy(src, dst, recv).start()

        @pl.when(jnp.logical_not(own))
        def _():
            remote(src, dst, send, recv, tok, ex).start()

    def sent(src, dst, send, recv, tok, ex):
        @pl.when(jnp.logical_not(jnp.logical_and(tok == t, ex == e)))
        def _():
            remote(src, dst, send, recv, tok, ex).wait_send()

    def landed(dst, recv):
        pltpu.make_async_copy(dst, dst, recv).wait()

    def rows(block, count=1):
        size = rows_dev * count
        return pl.ds(pl.multiple_of(block * size, size), size)

    barrier = pltpu.get_barrier_semaphore()

    def greet_plane(i):
        tok, ex = lax.div(i, 2), 2 * z + lax.rem(i, 2)

        @pl.when(jnp.logical_not(jnp.logical_and(tok == t, ex == e)))
        def _():
            pl.semaphore_signal(barrier, inc=1, device_id=(tok, ex), device_id_type=MESH)

    def greet_line(ex):
        @pl.when(lax.div(ex, 2) != z)
        def _():
            pl.semaphore_signal(barrier, inc=1, device_id=(t, ex), device_id_type=MESH)

    loop(2 * nt, greet_plane)
    loop(ne, greet_line)
    pl.semaphore_wait(barrier, 2 * nt - 1 + ne - 2)

    def line_copy(i):
        dz, half, core = lax.div(i, 4), lax.rem(lax.div(i, 2), 2), lax.rem(i, 2)
        plane = lax.rem(z + dz, nz)
        piece = (2 * plane + half) * 2 + core
        m = half * ne + e
        return (sw.at[piece], relay1.at[m], s1.at[i], r1.at[m], t, 2 * plane + core)

    def token_copy(i):
        place = lax.rem(q + i, ne)
        return (xs, xg.at[:, rows(t), :], st.at[i], tr.at[t], 2 * place + k, 2 * z + lax.rem(q, 2))

    def plane_copy(i):
        tok = lax.rem(t + i, nt)
        m = lax.rem(tok, 2) * ne + lax.div(tok, 2)
        return (relay1.at[m], ww.at[:, rows(t), :], s2.at[i], wr.at[t], tok, e)

    def twin_copy(i):
        block = 4 * lax.div(i, 2) + 2 * k + lax.rem(i, 2)
        part = xg.at[:, rows(block), :]
        return (part, part, sf.at[i], tr.at[block], t, sibling)

    prob_copy = remote(p2.at[1 - k], pr, ps, prs, t, sibling)
    prob_copy.start()
    loop(ne, lambda i: push(*token_copy(i)))
    loop(2 * ne, lambda i: push(*line_copy(i)))

    def forward_weights(i):
        src, dst, send, recv, tok, ex = plane_copy(i)
        m = lax.rem(tok, 2) * ne + lax.div(tok, 2)
        landed(src, r1.at[m])
        push(src, dst, send, recv, tok, ex)

    loop(nt, forward_weights)

    def forward_tokens(i):
        block = 4 * lax.div(i, 2) + 2 * k + lax.rem(i, 2)
        landed(xg.at[:, rows(block), :], tr.at[block])
        remote(*twin_copy(i)).start()

    loop(nt // 2, forward_tokens)

    def take_tokens(i):
        block = 4 * lax.div(i, 2) + 2 * (1 - k) + lax.rem(i, 2)
        landed(xg.at[:, rows(block), :], tr.at[block])

    loop(nt // 2, take_tokens)
    loop(nt, lambda i: landed(ww.at[:, rows(i), :], wr.at[i]))
    prob_copy.wait()
    loop(ne, lambda i: sent(*token_copy(i)))
    loop(2 * ne, lambda i: sent(*line_copy(i)))
    loop(nt, lambda i: sent(*plane_copy(i)))
    loop(nt // 2, lambda i: remote(*twin_copy(i)).wait_send())

    grow[...] = jnp.zeros_like(grow)
    mine = jnp.where(k == h, 1.0, 0.0).astype(F32)

    def hidden(hi):
        units = pl.ds(pl.multiple_of(hi * htile, htile), htile)
        wt[0] = ww[0, :, units].T
        wt[1] = ww[1, :, units].T

        def strip(ni):
            lanes = pl.ds(pl.multiple_of(ni * ntile, ntile), ntile)
            pre = jnp.dot(wt[0], xg[0, :, lanes], preferred_element_type=F32)
            hg = jnp.dot(wt[1], xg[1, :, lanes], preferred_element_type=F32)
            prob = p2[k, :, lanes] * mine + pr[:, lanes] * (1.0 - mine)
            sig = 1.0 / (1.0 + jnp.exp(-pre))
            act = (pre * sig).astype(BF16).astype(F32)
            slope = sig * (1.0 + pre * (1.0 - sig))
            pa[0, units, lanes] = (prob * hg * slope).astype(BF16)
            pa[1, units, lanes] = (prob * act).astype(BF16)
            grow[:, lanes] = grow[:, lanes] + jnp.sum(act * hg, axis=0, keepdims=True)

        loop(cols // ntile, strip)

    loop(hid // htile, hidden)

    def gate_copy(i):
        j = 2 * q + k
        return (grow, gpart.at[j], sg.at[i], gr.at[j], lax.rem(t + i, nt), column_core)

    loop(nt, lambda i: push(*gate_copy(i)))

    def grad_copy(block):
        m = h * ne + q
        return (dw.at[:, rows(block), :], relay2.at[m], sd.at[block], r2.at[m], block, e)

    def weight_grads(s):
        pair = lax.rem(q + s, ne)
        for a in range(2):
            dw[a, rows(pair, 2), :] = lax.dot_general(
                xg[a, rows(pair, 2), :], pa[a], (((1,), (1,)), ((), ())), preferred_element_type=F32
            ).astype(BF16)
        for w in range(2):
            push(*grad_copy(2 * pair + w))

    loop(ne, weight_grads)

    def pair_copy(u):
        pair = 2 * u + 1 - k
        return (xg.at[0, rows(pair, 2), :], cbuf.at[u], cs.at[u], cr.at[u], t, sibling)

    def block_copy(u, w):
        block = 2 * (2 * u + k) + w
        return (xg.at[0, rows(block), :], trecv.at[q], ts.at[2 * u + w], trr.at[q], block, column_core)

    def strips(pair, add):
        def strip(ni):
            lanes = pl.ds(pl.multiple_of(ni * ntile, ntile), ntile)
            part = jnp.dot(ww[0, rows(pair, 2), :], pa[0, :, lanes], preferred_element_type=F32)
            if add is not None:
                part = part + cbuf[add, :, lanes].astype(F32)
            xg[0, rows(pair, 2), lanes] = part.astype(BF16)

        loop(cols // ntile, strip)

    def give(u):
        strips(2 * u + 1 - k, None)
        remote(*pair_copy(u)).start()

    def keep(u):
        landed(cbuf.at[u], cr.at[u])
        strips(2 * u + k, u)
        for w in range(2):
            push(*block_copy(u, w))

    loop(ne // 2, give)
    loop(ne // 2, keep)

    def owner_copy(i):
        place, half = lax.rem(q + ne - lax.div(i, 2), ne), lax.rem(i, 2)
        piece = (2 * z + half) * 2 + k
        return (relay2.at[half * ne + place], wout.at[piece], fs.at[i], fr.at[piece], t, place)

    def forward_grads(i):
        place, half = lax.rem(q + ne - lax.div(i, 2), ne), lax.rem(i, 2)
        m = half * ne + place
        landed(relay2.at[m], r2.at[m])
        push(*owner_copy(i))

    loop(2 * ne, forward_grads)

    loop(2 * ne, lambda i: landed(wout.at[i], fr.at[i]))
    loop(ne, lambda i: landed(trecv.at[i], trr.at[i]))
    loop(nt, lambda i: landed(gpart.at[i], gr.at[i]))
    loop(nt, lambda i: sent(*gate_copy(i)))
    loop(nt, lambda i: sent(*grad_copy(i)))
    loop(ne // 2, lambda u: remote(*pair_copy(u)).wait_send())
    for w in range(2):
        loop(ne // 2, lambda u: sent(*block_copy(u, w)))
    loop(2 * ne, lambda i: sent(*owner_copy(i)))


def layer(sw, xs, p2, nt, ne):
    pieces, _, rows_dev, hid = sw.shape
    cols = xs.shape[2]
    width = nt * rows_dev
    htile, ntile = min(256, hid), min(512, cols)
    dma = pltpu.SemaphoreType.DMA
    anywhere = pl.BlockSpec(memory_space=pl.ANY)
    counts = (2 * ne, 2 * ne, ne, nt, nt, nt, nt // 2)
    counts_back = (nt, 2 * ne, nt, nt, ne // 2, ne // 2, ne, ne, 2 * ne, 2 * ne)
    return pl.pallas_call(
        functools.partial(layer_kernel, nt, ne, rows_dev, hid, cols, htile, ntile),
        out_shape=(
            jax.ShapeDtypeStruct(sw.shape, BF16),
            jax.ShapeDtypeStruct(sw.shape, BF16),
            jax.ShapeDtypeStruct(sw.shape, BF16),
            jax.ShapeDtypeStruct((ne, rows_dev, cols), BF16),
            jax.ShapeDtypeStruct((nt, 1, cols), F32),
        ),
        in_specs=[anywhere, anywhere, pl.BlockSpec(memory_space=pltpu.VMEM)],
        out_specs=(anywhere,) * 5,
        scratch_shapes=[
            pltpu.VMEM((2, width, cols), BF16),
            pltpu.VMEM((2, width, hid), BF16),
            pltpu.VMEM((2, hid, cols), BF16),
            pltpu.VMEM((2, width, hid), BF16),
            pltpu.VMEM((ne // 2, 2 * rows_dev, cols), BF16),
            pltpu.VMEM((2, htile, width), BF16),
            pltpu.VMEM((1, cols), F32),
            pltpu.VMEM((1, cols), F32),
            *[dma((count,)) for count in counts],
            dma,
            dma,
            *[dma((count,)) for count in counts_back],
        ],
        compiler_params=pltpu.CompilerParams(
            collective_id=0, has_side_effects=True, vmem_limit_bytes=60 * 1024 * 1024
        ),
        cost_estimate=pl.CostEstimate(
            flops=10 * width * hid * cols, bytes_accessed=64 << 20, transcendentals=hid * cols
        ),
    )(sw, xs, p2)


def combine_kernel(ids, pieces, up_out, down_out, total):
    total[...] = jnp.zeros_like(total)
    for n in range(pieces.shape[0]):
        expert = ids[n]
        for a in range(2):
            total[a, expert] = total[a, expert] + pieces[n, a].astype(F32)
    up_out[...] = total[0].astype(BF16)
    down_out[...] = total[1].astype(BF16)


def combine(ids, pieces, experts):
    count, _, rows_dev, hid = pieces.shape
    tile = 32 if rows_dev % 32 == 0 else 16
    out = jax.ShapeDtypeStruct((experts, rows_dev, hid), BF16)
    return pl.pallas_call(
        combine_kernel,
        out_shape=(out, out),
        grid_spec=pltpu.PrefetchScalarGridSpec(
            num_scalar_prefetch=1,
            grid=(rows_dev // tile,),
            in_specs=[pl.BlockSpec((count, 2, tile, hid), lambda i, ids: (0, 0, i, 0))],
            out_specs=[pl.BlockSpec((experts, tile, hid), lambda i, ids: (0, i, 0))] * 2,
            scratch_shapes=[pltpu.VMEM((2, experts, tile, hid), F32)],
        ),
        compiler_params=pltpu.CompilerParams(vmem_limit_bytes=32 * 1024 * 1024),
    )(ids, pieces)


def body(tokens, grad_out, gate_probs, routes, need_lists, up_weight, down_weight):
    nt, ne = lax.axis_size("tok"), lax.axis_size("exp")
    t, e = lax.axis_index("tok"), lax.axis_index("exp")
    experts = up_weight.shape[0]
    need = need_lists.reshape(ne, ne, nt // ne)
    ids = (jnp.take(need, e, axis=1) - e * experts).reshape(-1)
    sw = jnp.stack([jnp.take(up_weight, ids, axis=0), jnp.take(down_weight, ids, axis=0)], axis=1)
    xs = jnp.stack([tokens.T, grad_out.T])
    slots = 2 * (t // 2) + jnp.arange(2, dtype=jnp.int32)
    p2 = jnp.sum(jnp.where(routes[None] == slots[:, None, None], gate_probs[None], 0.0), axis=2)
    _, _, wout, trecv, gpart = layer(sw, xs, p2[:, None, :], nt, ne)
    token_grads = jnp.sum(trecv.astype(F32), axis=0).astype(BF16).T
    slot_ids = jnp.arange(nt, dtype=jnp.int32)
    hits = routes[None] == slot_ids[:, None, None]
    gate_grads = jnp.sum(jnp.where(hits, gpart.reshape(nt, -1, 1), 0.0), axis=0)
    up_grads, down_grads = combine(ids, wout, experts)
    return (token_grads, gate_grads, up_grads, down_grads)


def solution(mesh):
    split = (P("exp", "tok"), P("exp", "tok"), P("exp", None), P("exp", None))
    weights = P("exp", "tok", None)
    return jax.shard_map(
        body,
        mesh=mesh,
        in_specs=(*split, P(), weights, weights),
        out_specs=(P("exp", "tok"), P("exp", None), weights, weights),
        check_vma=False,
    )
```

time: 898 us -> 555 us (0.62)
  the two profiles are of different devices: /device:TPU:0 before, /device:TPU:56 now
where the time goes in v1:
time: 555 us; the launch traced here: 554 us
  Pallas kernels  521 us (94%)
  other arithmetic  20.7 us (4%)
  local copies, waits for them, and re-layouts  12.1 us (2%)
    pallas_call x1, Pallas kernels, layer(): pl.pallas_call(functools.partial(layer_kernel, nt, ne, rows_dev, hid, col...  516 us
    another operation x2, other arithmetic, body(): jnp.stack([jnp.take(up_weight, ids, axis=0), jnp.take(down_weight, ids, a...  12 us

profile of v1, /device:TPU:56, one launch (start us, length us, event | category | flops | bytes accessed | tf_op | source)
XLA Modules:
  0.0 554.3 jit_solution(14717393523615879051)
XLA Ops:
  0.6 0.0 copy-start
  0.7 0.9 copy.21
  1.6 0.1 copy.22
  1.7 0.1 sub.16.ids
  1.8 1.0 fusion
  2.8 0.6 broadcast_in_dim.55.p2
  3.4 2.5 pad_maximum_fusion.1.xs
  5.9 0.0 copy-done
  5.9 2.7 gather_fusion.1
  8.6 4.5 gather_fusion
  13.0 6.1 %select_bitcast_fusion.1 = (bf16[16,1,160,768]{3,2,1,0:T(8,128)(2,1)S(1)}, bf16[16,1,160,768]{3,2,1,0:T(8,128)(2,1)}) fusion(bf16[16,160,768]{2,1,0:T(8,128)(2,1)} %gather_fusion, pred[16]{0:T(512)(128)(4,1)S(1)} %compare_and_fusion, bf16[16,160,768]{2,1,0:T(8,128)(2,1)} %gather_fusion.1), kind=kLoop, calls=%fused_computation.4 | loop fusion | flops 3932160 | bytes 15728656 | tf_op jit(solution)/shard_map/stack | solution.py:315
  19.1 5.9 %pad_maximum_fusion.sw = bf16[16,2,160,768]{3,2,1,0:T(8,128)(2,1)} fusion(bf16[16,1,160,768]{3,2,1,0:T(8,128)(2,1)} %get-tuple-element.27, bf16[16,1,160,768]{3,2,1,0:T(8,128)(2,1)S(1)} %get-tuple-element.26), kind=kLoop, calls=%fused_computation.2 | loop fusion | flops 3932160 | bytes 15728640 | tf_op jit(solution)/shard_map/stack | solution.py:315
  25.0 515.5 %shard_map.102 = (bf16[16,2,160,768]{3,2,1,0:T(8,128)(2,1)}, bf16[16,2,160,768]{3,2,1,0:T(8,128)(2,1)}, bf16[16,2,160,768]{3,2,1,0:T(8,128)(2,1)}, bf16[8,160,2048]{2,1,0:T(8,128)(2,1)}, f32[16,1,2048]{2,1,0:T(1,128)}) custom-call(bf16[16,2,160,768]{3,2,1,0:T(8,128)(2,1)} %pad_maximum_fusion.sw, bf16[2,160,2048]{2,1,0:T(8,128)(2,1)} %pad_maximum_fusion.1.xs, ...), custom_call_target="tpu_custom_call" | custom-call | flops 40265318400 | bytes 67108864 | tf_op jit(solution)/shard_map/pallas_call | solution.py:247
  540.5 0.0 copy-start.3
  540.5 0.0 copy-start.2
  540.6 4.5 reduce_sum.31
  545.0 0.0 copy-done.3
  545.1 0.0 copy-done.2
  545.1 0.8 select_reduce_fusion
  545.9 0.0 copy-start.1
  545.9 3.2 copy-done.1
  549.1 5.2 shard_map.103
  (6 shorter events, 0.1 us)
Async XLA Ops:
  0.6 5.2 copy-start
  540.5 4.5 copy-start.3
  540.5 4.5 copy-start.2
  545.9 3.2 copy-start.1

commit v2 on v1

v2 whole, which is shorter than its diff:
```python
import functools

import jax
import jax.numpy as jnp
from jax import lax
from jax.experimental import pallas as pl
from jax.experimental.pallas import tpu as pltpu
from jax.sharding import PartitionSpec as P

MESH = pl.DeviceIdType.MESH
F32 = jnp.float32
BF16 = jnp.bfloat16


def loop(count, step, first=0):
    def run(i, carry):
        step(i)
        return carry

    lax.fori_loop(first, first + count, run, 0)


SIDE = 4
SHIFTS = (
    (2, 2), (1, 2), (3, 2), (2, 0), (0, 2), (1, 0), (3, 0), (0, 0),
    (2, 1), (2, 3), (1, 1), (3, 3), (1, 3), (3, 1), (0, 1), (0, 3),
)
LINE = (1, 3, 2, 0)


def pick(i, values):
    found = jnp.int32(0)
    for n, value in enumerate(values):
        found = jnp.where(i == n, value, found)
    return found


def shift(i):
    return pick(i, [dy for dy, _ in SHIFTS]), pick(i, [dx for _, dx in SHIFTS])


def layer_kernel(
    nt, ne, rows_dev, hid, cols, htile, ntile,
    su, sd, xt, gt, p2,
    relay1, relay2, wout, trecv, gpart,
    xg, ww, pa, pat, dw, cbuf, ring1, ring2, wt, pr, grow,
    s1, r1, sx, tr, sup, sdn, sf, s2, wr, ps, prs, s3, r2, sg, gr, cs, cr, qs, qr, ts, trr, fs, fr,
):
    t = lax.axis_index("tok")
    e = lax.axis_index("exp")
    z, k = lax.div(e, 2), lax.rem(e, 2)
    y, x = lax.div(t, SIDE), lax.rem(t, SIDE)
    q, h = lax.div(t, 2), lax.rem(t, 2)
    nz, ny = ne // 2, nt // SIDE
    sibling = 2 * z + 1 - k
    column_core = 2 * z + h
    above = lax.rem(y + 1, ny) * SIDE + x
    below = lax.rem(y + ny - 1, ny) * SIDE + x

    def remote(src, dst, send, recv, tok, ex):
        return pltpu.make_async_remote_copy(
            src_ref=src, dst_ref=dst, send_sem=send, recv_sem=recv,
            device_id=(tok, ex), device_id_type=MESH,
        )

    def push(src, dst, send, recv, tok, ex):
        own = jnp.logical_and(tok == t, ex == e)

        @pl.when(own)
        def _():
            pltpu.make_async_copy(src, dst, recv).start()

        @pl.when(jnp.logical_not(own))
        def _():
            remote(src, dst, send, recv, tok, ex).start()

    def sent(src, dst, send, recv, tok, ex):
        @pl.when(jnp.logical_not(jnp.logical_and(tok == t, ex == e)))
        def _():
            remote(src, dst, send, recv, tok, ex).wait_send()

    def landed(dst, recv):
        pltpu.make_async_copy(dst, dst, recv).wait()

    def place_of(tok):
        return lax.rem(tok, 2) * ne + lax.div(tok, 2)

    def rows(block):
        return pl.ds(pl.multiple_of(place_of(block) * rows_dev, rows_dev), rows_dev)

    def pair_rows(row, core):
        return pl.ds(pl.multiple_of((core * ne + 2 * row) * rows_dev, 2 * rows_dev), 2 * rows_dev)

    def target(i):
        dy, dx = shift(i)
        return lax.rem(y + dy, ny) * SIDE + lax.rem(x + dx, SIDE)

    def origin(i):
        dy, dx = shift(i)
        return lax.rem(y + ny - dy, ny) * SIDE + lax.rem(x + SIDE - dx, SIDE)

    barrier = pltpu.get_barrier_semaphore()

    def greet_plane(i):
        tok, ex = lax.div(i, 2), 2 * z + lax.rem(i, 2)

        @pl.when(jnp.logical_not(jnp.logical_and(tok == t, ex == e)))
        def _():
            pl.semaphore_signal(barrier, inc=1, device_id=(tok, ex), device_id_type=MESH)

    def greet_line(ex):
        @pl.when(lax.div(ex, 2) != z)
        def _():
            pl.semaphore_signal(barrier, inc=1, device_id=(t, ex), device_id_type=MESH)

    loop(2 * nt, greet_plane)
    loop(ne, greet_line)
    pl.semaphore_wait(barrier, 2 * nt - 1 + ne - 2)

    def token_part(a, block):
        return xg.at[a, rows(block), :]

    def row_copy(a, i):
        src = (xt, gt)[a]
        return (
            src, token_part(a, t), sx.at[2 * i + a], tr.at[2 * t + a],
            y * SIDE + k + 2 * i, column_core,
        )

    def ring_copy(a, block, sem, tok):
        part = token_part(a, block)
        return remote(part, part, sem, tr.at[2 * block + a], tok, e)

    def twin_copy(a, block, i):
        part = token_part(a, block)
        return remote(part, part, sf.at[2 * i + a], tr.at[2 * block + a], t, sibling)

    def row_block(dy, w):
        return lax.rem(y + dy, ny) * SIDE + k + 2 * w

    def line_copy(a, hs, i):
        half, core = lax.rem(x + hs, 2), lax.rem(i, 2)
        plane = lax.rem(z + pick(lax.div(i, 2), LINE), nz)
        piece = (2 * plane + half) * 2 + core
        m = half * ne + e
        src = (su, sd)[a]
        n = 2 * (ne * hs + i) + a
        return (src.at[piece], relay1.at[m, a], s1.at[n], r1.at[2 * m + a], t, 2 * plane + core)

    def plane_copy(a, i):
        tok = target(i)
        return (relay1.at[place_of(tok), a], ww.at[a, rows(t), :], s2.at[2 * i + a], wr.at[2 * t + a], tok, e)

    prob_copy = remote(p2.at[1 - k], pr, ps, prs, t, sibling)
    prob_copy.start()
    for a in range(2):
        loop(2, lambda i: push(*row_copy(a, i)))

    for hs in range(2):
        for a in range(2):
            loop(ne, lambda i: push(*line_copy(a, hs, i)))

    def forward_row(i):
        for a in range(2):
            block = row_block(0, i)
            landed(token_part(a, block), tr.at[2 * block + a])
            twin_copy(a, block, i).start()
            ring_copy(a, block, sup.at[2 * i + a], above).start()
            ring_copy(a, block, sdn.at[2 * i + a], below).start()

    loop(2, forward_row)

    def forward_ring():
        for a in range(2):
            lower, upper = row_block(ny - 1, 0), row_block(1, 1)
            landed(token_part(a, lower), tr.at[2 * lower + a])
            ring_copy(a, lower, sup.at[4 + a], above).start()
            twin_copy(a, lower, 2).start()
            landed(token_part(a, upper), tr.at[2 * upper + a])
            ring_copy(a, upper, sdn.at[4 + a], below).start()
            twin_copy(a, upper, 3).start()

    def forward_weights(hs, a):
        def step(i):
            m = place_of(target(i))
            landed(relay1.at[m, a], r1.at[2 * m + a])
            push(*plane_copy(a, i))

        loop(ne, step, hs * ne)

    forward_weights(0, 0)
    forward_weights(0, 1)
    forward_ring()
    forward_weights(1, 0)
    forward_weights(1, 1)

    late = ((ny - 1, 1), (1, 0), (2, 0), (2, 1))
    for n, (dy, w) in enumerate(late):
        for a in range(2):
            block = row_block(dy, w)
            landed(token_part(a, block), tr.at[2 * block + a])
            twin_copy(a, block, 4 + n).start()

    def take_tokens(i):
        block = 2 * i + 1 - k
        for a in range(2):
            landed(token_part(a, block), tr.at[2 * block + a])

    loop(nt // 2, take_tokens)
    for a in range(2):
        loop(nt, lambda i: landed(ww.at[a, rows(i), :], wr.at[2 * i + a]))
    prob_copy.wait()
    for a in range(2):
        loop(2, lambda i: sent(*row_copy(a, i)))
        for hs in range(2):
            loop(ne, lambda i: sent(*line_copy(a, hs, i)))
        loop(nt, lambda i: sent(*plane_copy(a, i)))
        for i in range(3):
            ring_copy(a, t, sup.at[2 * i + a], above).wait_send()
            ring_copy(a, t, sdn.at[2 * i + a], below).wait_send()
        loop(nt // 2, lambda i: twin_copy(a, t, i).wait_send())

    grow[...] = jnp.zeros_like(grow)
    mine = jnp.where(k == h, 1.0, 0.0).astype(F32)

    def hidden(hi):
        units = pl.ds(pl.multiple_of(hi * htile, htile), htile)
        wt[0] = ww[0, :, units].T
        wt[1] = ww[1, :, units].T

        def strip(ni):
            lanes = pl.ds(pl.multiple_of(ni * ntile, ntile), ntile)
            pre = jnp.dot(wt[0], xg[0, :, lanes], preferred_element_type=F32)
            hg = jnp.dot(wt[1], xg[1, :, lanes], preferred_element_type=F32)
            prob = p2[k, :, lanes] * mine + pr[:, lanes] * (1.0 - mine)
            sig = 1.0 / (1.0 + jnp.exp(-pre))
            act = (pre * sig).astype(BF16).astype(F32)
            slope = sig * (1.0 + pre * (1.0 - sig))
            grad = (prob * hg * slope).astype(BF16)
            pa[units, lanes] = grad
            pat[0, lanes, units] = grad.T
            pat[1, lanes, units] = (prob * act).astype(BF16).T
            grow[:, lanes] = grow[:, lanes] + jnp.sum(act * hg, axis=0, keepdims=True)

        loop(cols // ntile, strip)

    loop(hid // htile, hidden)

    def gate_copy(i):
        j = 2 * q + k
        return (grow, gpart.at[j], sg.at[i], gr.at[j], target(i), column_core)

    def grad_copy(a, i):
        block = target(i)
        m = h * ne + q
        src = ww.at[1, rows(block), :] if a == 0 else dw.at[rows(block), :]
        return (src, relay2.at[m, a], s3.at[2 * i + a], r2.at[2 * m + a], block, e)

    def weight_grads(i):
        part = rows(target(i))
        ww[1, part, :] = jnp.dot(xg[0, part, :], pat[0], preferred_element_type=F32).astype(BF16)
        push(*grad_copy(0, i))
        dw[part, :] = jnp.dot(xg[1, part, :], pat[1], preferred_element_type=F32).astype(BF16)
        push(*grad_copy(1, i))

    def owner_copy(i):
        tok = origin(i)
        piece = (2 * z + lax.rem(tok, 2)) * 2 + k
        return (relay2.at[place_of(tok)], wout.at[piece], fs.at[i], fr.at[piece], t, lax.div(tok, 2))

    def forward_grads(i):
        m = place_of(origin(i))
        for a in range(2):
            landed(relay2.at[m, a], r2.at[2 * m + a])
        push(*owner_copy(i))

    def row_at(dy):
        return lax.rem(y + dy, ny)

    def pair_copy(n, dy):
        row = row_at(dy)
        return remote(xg.at[0, pair_rows(row, 1 - k), :], cbuf.at[row], cs.at[n], cr.at[row], t, sibling)

    def give(n, dy):
        part = pair_rows(row_at(dy), 1 - k)
        xg[0, part, :] = jnp.dot(ww[0, part, :], pa[...], preferred_element_type=F32).astype(BF16)
        pair_copy(n, dy).start()

    def half_rows(row, w):
        return rows(row * SIDE + k + 2 * w)

    def keep(dy, added):
        row = row_at(dy)
        landed(cbuf.at[row], cr.at[row])
        for w in range(2):
            part = half_rows(row, w)
            total = jnp.dot(ww[0, part, :], pa[...], preferred_element_type=F32)
            total = total + cbuf[row, w * rows_dev:(w + 1) * rows_dev, :].astype(F32)
            for term in added[w]:
                total = total + term[...].astype(F32)
            xg[0, part, :] = total.astype(BF16)

    def far_copies():
        row = row_at(2)
        return (
            remote(xg.at[0, half_rows(row, 0), :], ring1.at[1], qs.at[0], qr.at[1], below, e),
            remote(xg.at[0, half_rows(row, 1), :], ring1.at[0], qs.at[1], qr.at[0], above, e),
        )

    def near_copy(n):
        src = xg.at[0, pair_rows(row_at((1, ny - 1)[n]), k), :]
        return remote(src, ring2.at[n], qs.at[2 + n], qr.at[2 + n], (above, below)[n], e)

    def row_owner(w):
        return (
            xg.at[0, half_rows(y, w), :], trecv.at[lax.div(x, 2)], ts.at[w], trr.at[lax.div(x, 2)],
            y * SIDE + k + 2 * w, column_core,
        )

    gives = (2, 1, ny - 1, 0)
    quarter = nt // 4
    loop(nt, weight_grads)
    loop(nt, lambda i: push(*gate_copy(i)))
    for n, dy in enumerate(gives):
        give(n, dy)
    keep(2, ((), ()))
    for copy in far_copies():
        copy.start()
    loop(quarter, forward_grads)
    landed(ring1.at[0], qr.at[0])
    keep(1, ((), (ring1.at[0],)))
    near_copy(0).start()
    loop(quarter, forward_grads, quarter)
    landed(ring1.at[1], qr.at[1])
    keep(ny - 1, ((ring1.at[1],), ()))
    near_copy(1).start()
    loop(quarter, forward_grads, 2 * quarter)
    for n in range(2):
        landed(ring2.at[n], qr.at[2 + n])
    both = [[ring2.at[n, pl.ds(w * rows_dev, rows_dev), :] for n in range(2)] for w in range(2)]
    keep(0, both)
    for w in range(2):
        push(*row_owner(w))
    loop(quarter, forward_grads, 3 * quarter)

    loop(2 * ne, lambda i: landed(wout.at[i], fr.at[i]))
    loop(2, lambda i: landed(trecv.at[i], trr.at[i]))
    loop(nt, lambda i: landed(gpart.at[i], gr.at[i]))
    loop(nt, lambda i: sent(*gate_copy(i)))
    for a in range(2):
        loop(nt, lambda i: sent(*grad_copy(a, i)))
    for n, dy in enumerate(gives):
        pair_copy(n, dy).wait_send()
    for copy in (*far_copies(), near_copy(0), near_copy(1)):
        copy.wait_send()
    for w in range(2):
        sent(*row_owner(w))
    loop(nt, lambda i: sent(*owner_copy(i)))


def layer(su, sd, xt, gt, p2, nt, ne):
    pieces, rows_dev, hid = su.shape
    cols = xt.shape[1]
    width = nt * rows_dev
    ny = nt // SIDE
    htile, ntile = min(256, hid), min(512, cols)
    dma = pltpu.SemaphoreType.DMA
    anywhere = pl.BlockSpec(memory_space=pl.ANY)
    relay = jax.ShapeDtypeStruct((pieces, 2, rows_dev, hid), BF16)
    counts = (4 * ne, 4 * ne, 4, 2 * nt, 6, 6, nt, 2 * nt, 2 * nt)
    counts_back = (2 * nt, 4 * ne, nt, nt, ny, ny, 4, 4, 2, 2, nt, 2 * ne)
    return pl.pallas_call(
        functools.partial(layer_kernel, nt, ne, rows_dev, hid, cols, htile, ntile),
        out_shape=(
            relay,
            relay,
            relay,
            jax.ShapeDtypeStruct((2, rows_dev, cols), BF16),
            jax.ShapeDtypeStruct((nt, 1, cols), F32),
        ),
        in_specs=[anywhere] * 4 + [pl.BlockSpec(memory_space=pltpu.VMEM)],
        out_specs=(anywhere,) * 5,
        scratch_shapes=[
            pltpu.VMEM((2, width, cols), BF16),
            pltpu.VMEM((2, width, hid), BF16),
            pltpu.VMEM((hid, cols), BF16),
            pltpu.VMEM((2, cols, hid), BF16),
            pltpu.VMEM((width, hid), BF16),
            pltpu.VMEM((ny, 2 * rows_dev, cols), BF16),
            pltpu.VMEM((2, rows_dev, cols), BF16),
            pltpu.VMEM((2, 2 * rows_dev, cols), BF16),
            pltpu.VMEM((2, htile, width), BF16),
            pltpu.VMEM((1, cols), F32),
            pltpu.VMEM((1, cols), F32),
            *[dma((count,)) for count in counts],
            dma,
            dma,
            *[dma((count,)) for count in counts_back],
        ],
        compiler_params=pltpu.CompilerParams(
            collective_id=0, has_side_effects=True, vmem_limit_bytes=60 * 1024 * 1024
        ),
        cost_estimate=pl.CostEstimate(
            flops=10 * width * hid * cols, bytes_accessed=64 << 20, transcendentals=hid * cols
        ),
    )(su, sd, xt, gt, p2)


def combine_kernel(ids, pieces, up_out, down_out, total):
    total[...] = jnp.zeros_like(total)
    for n in range(pieces.shape[0]):
        expert = ids[n]
        for a in range(2):
            total[a, expert] = total[a, expert] + pieces[n, a].astype(F32)
    up_out[...] = total[0].astype(BF16)
    down_out[...] = total[1].astype(BF16)


def combine(ids, pieces, experts):
    count, _, rows_dev, hid = pieces.shape
    tile = 32 if rows_dev % 32 == 0 else 16
    out = jax.ShapeDtypeStruct((experts, rows_dev, hid), BF16)
    return pl.pallas_call(
        combine_kernel,
        out_shape=(out, out),
        grid_spec=pltpu.PrefetchScalarGridSpec(
            num_scalar_prefetch=1,
            grid=(rows_dev // tile,),
            in_specs=[pl.BlockSpec((count, 2, tile, hid), lambda i, ids: (0, 0, i, 0))],
            out_specs=[pl.BlockSpec((experts, tile, hid), lambda i, ids: (0, i, 0))] * 2,
            scratch_shapes=[pltpu.VMEM((2, experts, tile, hid), F32)],
        ),
        compiler_params=pltpu.CompilerParams(vmem_limit_bytes=32 * 1024 * 1024),
    )(ids, pieces)


def body(tokens, grad_out, gate_probs, routes, need_lists, up_weight, down_weight):
    nt, ne = lax.axis_size("tok"), lax.axis_size("exp")
    t, e = lax.axis_index("tok"), lax.axis_index("exp")
    experts = up_weight.shape[0]
    need = need_lists.reshape(ne, ne, nt // ne)
    ids = (jnp.take(need, e, axis=1) - e * experts).reshape(-1)
    su = up_weight.at[ids].get(mode="promise_in_bounds")
    sd = down_weight.at[ids].get(mode="promise_in_bounds")
    slots = 2 * (t // 2) + jnp.arange(2, dtype=jnp.int32)
    p2 = jnp.sum(jnp.where(routes[None] == slots[:, None, None], gate_probs[None], 0.0), axis=2)
    _, _, wout, trecv, gpart = layer(su, sd, tokens.T, grad_out.T, p2[:, None, :], nt, ne)
    token_grads = jnp.sum(trecv.astype(F32), axis=0).astype(BF16).T
    slot_ids = jnp.arange(nt, dtype=jnp.int32)
    hits = routes[None] == slot_ids[:, None, None]
    gate_grads = jnp.sum(jnp.where(hits, gpart.reshape(nt, -1, 1), 0.0), axis=0)
    up_grads, down_grads = combine(ids, wout, experts)
    return (token_grads, gate_grads, up_grads, down_grads)


def solution(mesh):
    split = (P("exp", "tok"), P("exp", "tok"), P("exp", None), P("exp", None))
    weights = P("exp", "tok", None)
    return jax.shard_map(
        body,
        mesh=mesh,
        in_specs=(*split, P(), weights, weights),
        out_specs=(P("exp", "tok"), P("exp", None), weights, weights),
        check_vma=False,
    )
```

time: 555 us -> 434 us (0.78)
  the two profiles are of different devices: /device:TPU:56 before, /device:TPU:0 now
where the time goes in v2:
time: 434 us; the launch traced here: 433 us
  Pallas kernels  415 us (96%)
  local copies, waits for them, and re-layouts  13.2 us (3%)
  other arithmetic  4.41 us (1%)
    pallas_call x1, Pallas kernels, layer(): pl.pallas_call(functools.partial(layer_kernel, nt, ne, rows_dev, hid, col...  410 us

profile of v2, /device:TPU:0, one launch (start us, length us, event | category | flops | bytes accessed | tf_op | source)
XLA Modules:
  0.0 433.3 jit_solution(6640312834419348725)
XLA Ops:
  0.6 0.0 copy-start
  0.7 0.9 copy.23
  1.6 0.1 copy.24
  1.7 0.1 sub.28.ids
  1.8 0.1 sub.26
  1.9 1.0 fusion
  2.9 0.6 broadcast_in_dim.48.p2
  3.5 0.0 copy-done
  3.5 2.8 gather_fusion.1
  6.3 4.4 %gather_fusion = bf16[16,160,768]{2,1,0:T(8,128)(2,1)} fusion(bf16[10,160,768]{2,1,0:T(8,128)(2,1)} %param.12, s32[1024]{0:T(1024)S(1)} %pad_clamp_fusion), kind=kCustom, calls=%fused_computation | custom fusion | bytes 7864384 | tf_op jit(solution)/shard_map/gather | solution.py:443
  10.7 0.0 copy-start.2
  10.7 409.8 %shard_map.102 = (bf16[16,2,160,768]{3,2,1,0:T(8,128)(2,1)}, bf16[16,2,160,768]{3,2,1,0:T(8,128)(2,1)}, bf16[16,2,160,768]{3,2,1,0:T(8,128)(2,1)}, bf16[2,160,2048]{2,1,0:T(8,128)(2,1)}, f32[16,1,2048]{2,1,0:T(1,128)}) custom-call(bf16[16,160,768]{2,1,0:T(8,128)(2,1)} %gather_fusion, bf16[16,160,768]{2,1,0:T(8,128)(2,1)} %gather_fusion.1, ...), custom_call_target="tpu_custom_call" | custom-call | flops 40265318400 | bytes 67108864 | tf_op jit(solution)/shard_map/pallas_call | solution.py:372
  420.5 2.6 reduce_sum.31
  423.1 0.9 copy.28
  424.1 0.0 copy-done.2
  424.1 0.8 select_reduce_fusion
  424.9 0.0 copy-start.1
  424.9 3.2 copy-done.1
  428.1 5.2 %shard_map.103 = (bf16[10,160,768]{2,1,0:T(8,128)(2,1)}, bf16[10,160,768]{2,1,0:T(8,128)(2,1)}) custom-call(s32[16]{0:T(128)S(1)} %sub.28.ids, bf16[16,2,160,768]{3,2,1,0:T(8,128)(2,1)S(1)} %copy-done.1), custom_call_target="tpu_custom_call" | custom-call | tf_op jit(solution)/shard_map/pallas_call | solution.py:423
  (4 shorter events, 0.0 us)
Async XLA Ops:
  0.6 2.9 copy-start
  10.7 413.3 %copy-start.2 = (s32[2048,6]{0,1:T(8,128)S(1)}, s32[2048,6]{0,1:T(8,128)}, u32[]{:S(2)}) copy-start(s32[2048,6]{0,1:T(8,128)} %param.10) | copy-start | bytes 147460
  424.9 3.2 copy-start.1

commit v3 on v2

--- a/solution.py
+++ b/solution.py
@@ -26,6 +26,7 @@
     (2, 1), (2, 3), (1, 1), (3, 3), (1, 3), (3, 1), (0, 1), (0, 3),
 )
 LINE = (1, 3, 2, 0)
+PARTS = 3
 
 
 def pick(i, values):
@@ -41,7 +42,7 @@
 
 def layer_kernel(
     nt, ne, rows_dev, hid, cols, htile, ntile,
-    su, sd, xt, gt, p2,
+    sw, xt, gt, p2,
     relay1, relay2, wout, trecv, gpart,
     xg, ww, pa, pat, dw, cbuf, ring1, ring2, wt, pr, grow,
     s1, r1, sx, tr, sup, sdn, sf, s2, wr, ps, prs, s3, r2, sg, gr, cs, cr, qs, qr, ts, trr, fs, fr,
@@ -138,27 +139,32 @@
     def row_block(dy, w):
         return lax.rem(y + dy, ny) * SIDE + k + 2 * w
 
-    def line_copy(a, hs, i):
-        half, core = lax.rem(x + hs, 2), lax.rem(i, 2)
-        plane = lax.rem(z + pick(lax.div(i, 2), LINE), nz)
+    def line_copy(s, i):
+        hs, j = lax.div(i, ne), lax.rem(i, ne)
+        half, core = lax.rem(x + hs, 2), lax.rem(j, 2)
+        plane = lax.rem(z + pick(lax.div(j, 2), LINE), nz)
         piece = (2 * plane + half) * 2 + core
         m = half * ne + e
-        src = (su, sd)[a]
-        n = 2 * (ne * hs + i) + a
-        return (src.at[piece], relay1.at[m, a], s1.at[n], r1.at[2 * m + a], t, 2 * plane + core)
-
-    def plane_copy(a, i):
+        return (
+            sw.at[piece, s], relay1.at[m, s], s1.at[2 * ne * s + i], r1.at[2 * ne * s + m], t, 2 * plane + core,
+        )
+
+    def plane_copy(s, i):
         tok = target(i)
-        return (relay1.at[place_of(tok), a], ww.at[a, rows(t), :], s2.at[2 * i + a], wr.at[2 * t + a], tok, e)
+        return (
+            relay1.at[place_of(tok), s], ww.at[s, :, rows(t), :], s2.at[nt * s + i], wr.at[nt * s + t], tok, e,
+        )
 
     prob_copy = remote(p2.at[1 - k], pr, ps, prs, t, sibling)
     prob_copy.start()
     for a in range(2):
         loop(2, lambda i: push(*row_copy(a, i)))
 
-    for hs in range(2):
-        for a in range(2):
-            loop(ne, lambda i: push(*line_copy(a, hs, i)))
+    def send_line(s):
+        loop(2 * ne, lambda i: push(*line_copy(s, i)))
+
+    send_line(0)
+    send_line(1)
 
     def forward_row(i):
         for a in range(2):
@@ -167,8 +173,6 @@
             twin_copy(a, block, i).start()
             ring_copy(a, block, sup.at[2 * i + a], above).start()
             ring_copy(a, block, sdn.at[2 * i + a], below).start()
-
-    loop(2, forward_row)
 
     def forward_ring():
         for a in range(2):
@@ -180,20 +184,19 @@
             ring_copy(a, upper, sdn.at[4 + a], below).start()
             twin_copy(a, upper, 3).start()
 
-    def forward_weights(hs, a):
+    def forward_weights(s):
         def step(i):
             m = place_of(target(i))
-            landed(relay1.at[m, a], r1.at[2 * m + a])
-            push(*plane_copy(a, i))
-
-        loop(ne, step, hs * ne)
-
-    forward_weights(0, 0)
-    forward_weights(0, 1)
+            landed(relay1.at[m, s], r1.at[2 * ne * s + m])
+            push(*plane_copy(s, i))
+
+        loop(nt, step)
+
+    loop(2, forward_row)
+    forward_weights(0)
+    send_line(2)
     forward_ring()
-    forward_weights(1, 0)
-    forward_weights(1, 1)
-
+    forward_weights(1)
     late = ((ny - 1, 1), (1, 0), (2, 0), (2, 1))
     for n, (dy, w) in enumerate(late):
         for a in range(2):
@@ -201,32 +204,24 @@
             landed(token_part(a, block), tr.at[2 * block + a])
             twin_copy(a, block, 4 + n).start()
 
+    forward_weights(2)
+
     def take_tokens(i):
         block = 2 * i + 1 - k
         for a in range(2):
             landed(token_part(a, block), tr.at[2 * block + a])
 
     loop(nt // 2, take_tokens)
-    for a in range(2):
-        loop(nt, lambda i: landed(ww.at[a, rows(i), :], wr.at[2 * i + a]))
     prob_copy.wait()
-    for a in range(2):
-        loop(2, lambda i: sent(*row_copy(a, i)))
-        for hs in range(2):
-            loop(ne, lambda i: sent(*line_copy(a, hs, i)))
-        loop(nt, lambda i: sent(*plane_copy(a, i)))
-        for i in range(3):
-            ring_copy(a, t, sup.at[2 * i + a], above).wait_send()
-            ring_copy(a, t, sdn.at[2 * i + a], below).wait_send()
-        loop(nt // 2, lambda i: twin_copy(a, t, i).wait_send())
 
     grow[...] = jnp.zeros_like(grow)
     mine = jnp.where(k == h, 1.0, 0.0).astype(F32)
 
-    def hidden(hi):
-        units = pl.ds(pl.multiple_of(hi * htile, htile), htile)
-        wt[0] = ww[0, :, units].T
-        wt[1] = ww[1, :, units].T
+    def hidden(s):
+        units = pl.ds(s * htile, htile)
+        loop(nt, lambda i: landed(ww.at[s, :, rows(i), :], wr.at[nt * s + i]))
+        wt[0] = ww[s, 0].T
+        wt[1] = ww[s, 1].T
 
         def strip(ni):
             lanes = pl.ds(pl.multiple_of(ni * ntile, ntile), ntile)
@@ -238,44 +233,52 @@
             slope = sig * (1.0 + pre * (1.0 - sig))
             grad = (prob * hg * slope).astype(BF16)
             pa[units, lanes] = grad
-            pat[0, lanes, units] = grad.T
-            pat[1, lanes, units] = (prob * act).astype(BF16).T
+            pat[0, lanes, :] = grad.T
+            pat[1, lanes, :] = (prob * act).astype(BF16).T
             grow[:, lanes] = grow[:, lanes] + jnp.sum(act * hg, axis=0, keepdims=True)
 
         loop(cols // ntile, strip)
-
-    loop(hid // htile, hidden)
 
     def gate_copy(i):
         j = 2 * q + k
         return (grow, gpart.at[j], sg.at[i], gr.at[j], target(i), column_core)
 
-    def grad_copy(a, i):
+    def grad_copy(s, i):
         block = target(i)
         m = h * ne + q
-        src = ww.at[1, rows(block), :] if a == 0 else dw.at[rows(block), :]
-        return (src, relay2.at[m, a], s3.at[2 * i + a], r2.at[2 * m + a], block, e)
-
-    def weight_grads(i):
-        part = rows(target(i))
-        ww[1, part, :] = jnp.dot(xg[0, part, :], pat[0], preferred_element_type=F32).astype(BF16)
-        push(*grad_copy(0, i))
-        dw[part, :] = jnp.dot(xg[1, part, :], pat[1], preferred_element_type=F32).astype(BF16)
-        push(*grad_copy(1, i))
-
-    def owner_copy(i):
+        return (dw.at[s, :, rows(block), :], relay2.at[m, s], s3.at[nt * s + i], r2.at[2 * ne * s + m], block, e)
+
+    def weight_grads(s):
+        def step(i):
+            part = rows(target(i))
+            for a in range(2):
+                dw[s, a, part, :] = jnp.dot(xg[a, part, :], pat[a], preferred_element_type=F32).astype(BF16)
+            push(*grad_copy(s, i))
+
+        loop(nt, step)
+
+    def owner_copy(s, i):
         tok = origin(i)
         piece = (2 * z + lax.rem(tok, 2)) * 2 + k
-        return (relay2.at[place_of(tok)], wout.at[piece], fs.at[i], fr.at[piece], t, lax.div(tok, 2))
-
-    def forward_grads(i):
-        m = place_of(origin(i))
-        for a in range(2):
-            landed(relay2.at[m, a], r2.at[2 * m + a])
-        push(*owner_copy(i))
+        return (
+            relay2.at[place_of(tok), s], wout.at[piece, s], fs.at[nt * s + i], fr.at[2 * ne * s + piece],
+            t, lax.div(tok, 2),
+        )
+
+    def forward_grads(s, count=nt, first=0):
+        def step(i):
+            m = place_of(origin(i))
+            landed(relay2.at[m, s], r2.at[2 * ne * s + m])
+            push(*owner_copy(s, i))
+
+        loop(count, step, first)
 
     def row_at(dy):
         return lax.rem(y + dy, ny)
+
+    def token_part_grads(part):
+        weights = jnp.concatenate([ww[s, 0, part, :] for s in range(PARTS)], axis=1)
+        return jnp.dot(weights, pa[...], preferred_element_type=F32)
 
     def pair_copy(n, dy):
         row = row_at(dy)
@@ -283,7 +286,7 @@
 
     def give(n, dy):
         part = pair_rows(row_at(dy), 1 - k)
-        xg[0, part, :] = jnp.dot(ww[0, part, :], pa[...], preferred_element_type=F32).astype(BF16)
+        xg[0, part, :] = token_part_grads(part).astype(BF16)
         pair_copy(n, dy).start()
 
     def half_rows(row, w):
@@ -294,7 +297,7 @@
         landed(cbuf.at[row], cr.at[row])
         for w in range(2):
             part = half_rows(row, w)
-            total = jnp.dot(ww[0, part, :], pa[...], preferred_element_type=F32)
+            total = token_part_grads(part)
             total = total + cbuf[row, w * rows_dev:(w + 1) * rows_dev, :].astype(F32)
             for term in added[w]:
                 total = total + term[...].astype(F32)
@@ -319,56 +322,73 @@
 
     gives = (2, 1, ny - 1, 0)
     quarter = nt // 4
-    loop(nt, weight_grads)
+    last = PARTS - 1
+    for s in range(PARTS):
+        hidden(s)
+        weight_grads(s)
+        if s == last:
+            break
+    forward_grads(0)
     loop(nt, lambda i: push(*gate_copy(i)))
+    for a in range(2):
+        for i in range(3):
+            ring_copy(a, t, sup.at[2 * i + a], above).wait_send()
+            ring_copy(a, t, sdn.at[2 * i + a], below).wait_send()
+        loop(nt // 2, lambda i: twin_copy(a, t, i).wait_send())
     for n, dy in enumerate(gives):
         give(n, dy)
     keep(2, ((), ()))
     for copy in far_copies():
         copy.start()
-    loop(quarter, forward_grads)
+    forward_grads(last - 1)
     landed(ring1.at[0], qr.at[0])
     keep(1, ((), (ring1.at[0],)))
     near_copy(0).start()
-    loop(quarter, forward_grads, quarter)
+    forward_grads(last, quarter)
     landed(ring1.at[1], qr.at[1])
     keep(ny - 1, ((ring1.at[1],), ()))
     near_copy(1).start()
-    loop(quarter, forward_grads, 2 * quarter)
+    forward_grads(last, 2 * quarter, quarter)
     for n in range(2):
         landed(ring2.at[n], qr.at[2 + n])
     both = [[ring2.at[n, pl.ds(w * rows_dev, rows_dev), :] for n in range(2)] for w in range(2)]
     keep(0, both)
     for w in range(2):
         push(*row_owner(w))
-    loop(quarter, forward_grads, 3 * quarter)
-
-    loop(2 * ne, lambda i: landed(wout.at[i], fr.at[i]))
+    forward_grads(last, quarter, 3 * quarter)
+
+    for s in range(PARTS):
+        loop(2 * ne, lambda i: landed(wout.at[i, s], fr.at[2 * ne * s + i]))
     loop(2, lambda i: landed(trecv.at[i], trr.at[i]))
     loop(nt, lambda i: landed(gpart.at[i], gr.at[i]))
     loop(nt, lambda i: sent(*gate_copy(i)))
     for a in range(2):
-        loop(nt, lambda i: sent(*grad_copy(a, i)))
+        loop(2, lambda i: sent(*row_copy(a, i)))
+    for s in range(PARTS):
+        loop(2 * ne, lambda i: sent(*line_copy(s, i)))
+        loop(nt, lambda i: sent(*plane_copy(s, i)))
+        loop(nt, lambda i: sent(*grad_copy(s, i)))
+        loop(nt, lambda i: sent(*owner_copy(s, i)))
     for n, dy in enumerate(gives):
         pair_copy(n, dy).wait_send()
     for copy in (*far_copies(), near_copy(0), near_copy(1)):
         copy.wait_send()
     for w in range(2):
         sent(*row_owner(w))
-    loop(nt, lambda i: sent(*owner_copy(i)))
-
-
-def layer(su, sd, xt, gt, p2, nt, ne):
-    pieces, rows_dev, hid = su.shape
+
+
+def layer(sw, xt, gt, p2, nt, ne):
+    _, _, _, rows_dev, htile = sw.shape
+    hid = PARTS * htile
     cols = xt.shape[1]
     width = nt * rows_dev
     ny = nt // SIDE
-    htile, ntile = min(256, hid), min(512, cols)
+    ntile = min(512, cols)
     dma = pltpu.SemaphoreType.DMA
     anywhere = pl.BlockSpec(memory_space=pl.ANY)
-    relay = jax.ShapeDtypeStruct((pieces, 2, rows_dev, hid), BF16)
-    counts = (4 * ne, 4 * ne, 4, 2 * nt, 6, 6, nt, 2 * nt, 2 * nt)
-    counts_back = (2 * nt, 4 * ne, nt, nt, ny, ny, 4, 4, 2, 2, nt, 2 * ne)
+    relay = jax.ShapeDtypeStruct(sw.shape, BF16)
+    counts = (6 * ne, 6 * ne, 4, 2 * nt, 6, 6, nt, 3 * nt, 3 * nt)
+    counts_back = (3 * nt, 6 * ne, nt, nt, ny, ny, 4, 4, 2, 2, 3 * nt, 6 * ne)
     return pl.pallas_call(
         functools.partial(layer_kernel, nt, ne, rows_dev, hid, cols, htile, ntile),
         out_shape=(
@@ -378,14 +398,14 @@
             jax.ShapeDtypeStruct((2, rows_dev, cols), BF16),
             jax.ShapeDtypeStruct((nt, 1, cols), F32),
         ),
-        in_specs=[anywhere] * 4 + [pl.BlockSpec(memory_space=pltpu.VMEM)],
+        in_specs=[anywhere] * 3 + [pl.BlockSpec(memory_space=pltpu.VMEM)],
         out_specs=(anywhere,) * 5,
         scratch_shapes=[
             pltpu.VMEM((2, width, cols), BF16),
-            pltpu.VMEM((2, width, hid), BF16),
+            pltpu.VMEM((PARTS, 2, width, htile), BF16),
             pltpu.VMEM((hid, cols), BF16),
-            pltpu.VMEM((2, cols, hid), BF16),
-            pltpu.VMEM((width, hid), BF16),
+            pltpu.VMEM((2, cols, htile), BF16),
+            pltpu.VMEM((PARTS, 2, width, htile), BF16),
             pltpu.VMEM((ny, 2 * rows_dev, cols), BF16),
             pltpu.VMEM((2, rows_dev, cols), BF16),
             pltpu.VMEM((2, 2 * rows_dev, cols), BF16),
@@ -403,21 +423,48 @@
         cost_estimate=pl.CostEstimate(
             flops=10 * width * hid * cols, bytes_accessed=64 << 20, transcendentals=hid * cols
         ),
-    )(su, sd, xt, gt, p2)
+    )(sw, xt, gt, p2)
+
+
+def take_kernel(ids, up, down, out):
+    htile = out.shape[-1]
+    for s in range(PARTS):
+        for a, weight in enumerate((up, down)):
+            out[0, s, a] = weight[0, :, s * htile:(s + 1) * htile]
+
+
+def take(ids, up_weight, down_weight):
+    _, rows_dev, hid = up_weight.shape
+    count = ids.shape[0]
+    block = (1, PARTS, 2, rows_dev, hid // PARTS)
+    return pl.pallas_call(
+        take_kernel,
+        out_shape=jax.ShapeDtypeStruct((count, *block[1:]), BF16),
+        grid_spec=pltpu.PrefetchScalarGridSpec(
+            num_scalar_prefetch=1,
+            grid=(count,),
+            in_specs=[pl.BlockSpec((1, rows_dev, hid), lambda i, ids: (ids[i], 0, 0))] * 2,
+            out_specs=pl.BlockSpec(block, lambda i, ids: (i, 0, 0, 0, 0)),
+        ),
+    )(ids, up_weight, down_weight)
 
 
 def combine_kernel(ids, pieces, up_out, down_out, total):
+    htile = pieces.shape[-1]
     total[...] = jnp.zeros_like(total)
     for n in range(pieces.shape[0]):
         expert = ids[n]
-        for a in range(2):
-            total[a, expert] = total[a, expert] + pieces[n, a].astype(F32)
+        for s in range(PARTS):
+            units = slice(s * htile, (s + 1) * htile)
+            for a in range(2):
+                total[a, expert, :, units] = total[a, expert, :, units] + pieces[n, s, a].astype(F32)
     up_out[...] = total[0].astype(BF16)
     down_out[...] = total[1].astype(BF16)
 
 
 def combine(ids, pieces, experts):
-    count, _, rows_dev, hid = pieces.shape
+    count, parts, _, rows_dev, htile = pieces.shape
+    hid = parts * htile
     tile = 32 if rows_dev % 32 == 0 else 16
     out = jax.ShapeDtypeStruct((experts, rows_dev, hid), BF16)
     return pl.pallas_call(
@@ -426,7 +473,7 @@
         grid_spec=pltpu.PrefetchScalarGridSpec(
             num_scalar_prefetch=1,
             grid=(rows_dev // tile,),
-            in_specs=[pl.BlockSpec((count, 2, tile, hid), lambda i, ids: (0, 0, i, 0))],
+            in_specs=[pl.BlockSpec((count, parts, 2, tile, htile), lambda i, ids: (0, 0, 0, i, 0))],
             out_specs=[pl.BlockSpec((experts, tile, hid), lambda i, ids: (0, i, 0))] * 2,
             scratch_shapes=[pltpu.VMEM((2, experts, tile, hid), F32)],
         ),
@@ -440,11 +487,10 @@
     experts = up_weight.shape[0]
     need = need_lists.reshape(ne, ne, nt // ne)
     ids = (jnp.take(need, e, axis=1) - e * experts).reshape(-1)
-    su = up_weight.at[ids].get(mode="promise_in_bounds")
-    sd = down_weight.at[ids].get(mode="promise_in_bounds")
+    sw = take(ids, up_weight, down_weight)
     slots = 2 * (t // 2) + jnp.arange(2, dtype=jnp.int32)
     p2 = jnp.sum(jnp.where(routes[None] == slots[:, None, None], gate_probs[None], 0.0), axis=2)
-    _, _, wout, trecv, gpart = layer(su, sd, tokens.T, grad_out.T, p2[:, None, :], nt, ne)
+    _, _, wout, trecv, gpart = layer(sw, tokens.T, grad_out.T, p2[:, None, :], nt, ne)
     token_grads = jnp.sum(trecv.astype(F32), axis=0).astype(BF16).T
     slot_ids = jnp.arange(nt, dtype=jnp.int32)
     hits = routes[None] == slot_ids[:, None, None]

time: 434 us -> 398 us (0.917); the launches traced: 433 us -> 390 us
  Pallas kernels: 415 us -> 379 us
  local copies, waits for them, and re-layouts: 13.2 us -> 6.24 us
    pallas_call x1, Pallas kernels: 410 us -> 361 us  [layer(): pl.pallas_call(functools.partial(layer_kernel, nt, ne, rows_dev, hid, col...]
    pallas_call x0 -> x1, Pallas kernels: none -> 12.8 us  [take(): pl.pallas_call(take_kernel, out_shape=jax.ShapeDtypeStruct((count, *block...]
    gather x2 -> x0, local copies, waits for them, and re-layouts: 7.24 us -> none  [the longest x1 4.44 us: body(): su = up_weight.at[ids].get(mode='promise_in_bounds')]
where the time goes in v3:
time: 398 us; the launch traced here: 390 us
  Pallas kernels  379 us (95%)
  local copies, waits for them, and re-layouts  6.24 us (2%)
  other arithmetic  4.39 us (1%)
    pallas_call x1, Pallas kernels, layer(): pl.pallas_call(functools.partial(layer_kernel, nt, ne, rows_dev, hid, col...  361 us
    pallas_call x1, Pallas kernels, take(): pl.pallas_call(take_kernel, out_shape=jax.ShapeDtypeStruct((count, *block...  12.8 us

profile of v3, /device:TPU:0, one launch (start us, length us, event | category | flops | bytes accessed | tf_op | source)
XLA Modules:
  0.0 390.4 jit_solution(12632642187600451762)
XLA Ops:
  0.7 0.8 copy.21
  1.4 0.1 copy.22
  1.5 0.6 sub.16.ids
  2.1 1.0 fusion
  3.1 0.6 broadcast_in_dim.46.p2
  3.7 12.8 %shard_map.102.sw = bf16[16,3,2,160,256]{4,3,2,1,0:T(8,128)(2,1)} custom-call(s32[16]{0:T(128)} %sub.16.ids, bf16[10,160,768]{2,1,0:T(8,128)(2,1)} %up.1, bf16[10,160,768]{2,1,0:T(8,128)(2,1)} %down.1), custom_call_target="tpu_custom_call" | custom-call | tf_op jit(solution)/shard_map/pallas_call | solution.py:440
  16.5 0.0 copy-start.2
  16.5 361.1 %shard_map.103 = (bf16[16,3,2,160,256]{4,3,2,1,0:T(8,128)(2,1)}, bf16[16,3,2,160,256]{4,3,2,1,0:T(8,128)(2,1)}, bf16[16,3,2,160,256]{4,3,2,1,0:T(8,128)(2,1)}, b...) custom-call(bf16[16,3,2,160,256]{4,3,2,1,0:T(8,128)(2,1)} %shard_map.102.sw, bf16[160,2048]{1,0:T(8,128)(2,1)} %bitcast.12, ...), custom_call_target="tpu_custom_call" | custom-call | flops 40265318400 | bytes 67108864 | tf_op jit(solution)/shard_map/pallas_call | solution.py:392
  377.6 0.0 copy-start.1
  377.6 2.6 reduce_sum.31
  380.2 0.9 copy.25
  381.1 0.0 copy-done.2
  381.2 0.8 select_reduce_fusion
  382.0 0.0 copy-done.1
  382.0 0.0 copy-start
  382.0 3.2 copy-done
  385.2 5.2 %shard_map.104 = (bf16[10,160,768]{2,1,0:T(8,128)(2,1)}, bf16[10,160,768]{2,1,0:T(8,128)(2,1)}) custom-call(s32[16]{0:T(128)S(1)} %copy-done.1, bf16[16,3,2,160,256]{4,3,2,1,0:T(8,128)(2,1)S(1)} %copy-done), custom_call_target="tpu_custom_call" | custom-call | tf_op jit(solution)/shard_map/pallas_call | solution.py:470
  (2 shorter events, 0.0 us)
Async XLA Ops:
  16.5 364.6 %copy-start.2 = (s32[2048,6]{0,1:T(8,128)S(1)}, s32[2048,6]{0,1:T(8,128)}, u32[]{:S(2)}) copy-start(s32[2048,6]{0,1:T(8,128)} %param.10) | copy-start | bytes 147460
  377.6 4.4 %copy-start.1 = (s32[16]{0:T(128)S(1)}, s32[16]{0:T(128)}, u32[]{:S(2)}) copy-start(s32[16]{0:T(128)} %sub.16.ids) | copy-start | bytes 196
  382.0 3.2 copy-start

commit v4 on v3

--- a/solution.py
+++ b/solution.py
@@ -43,9 +43,9 @@
 def layer_kernel(
     nt, ne, rows_dev, hid, cols, htile, ntile,
     sw, xt, gt, p2,
-    relay1, relay2, wout, trecv, gpart,
-    xg, ww, pa, pat, dw, cbuf, ring1, ring2, wt, pr, grow,
-    s1, r1, sx, tr, sup, sdn, sf, s2, wr, ps, prs, s3, r2, sg, gr, cs, cr, qs, qr, ts, trr, fs, fr,
+    relay1, relay2, wout, trecv, gpart, gstage,
+    xg, ww, pa, pat, dw, cbuf, ring1, ring2, spare, wt, pr, grow,
+    s1, r1, sx, tr, sup, sdn, sf, gs, gq, gx, s2, wr, ps, prs, s3, r2, sg, gr, cs, cr, qs, qr, ts, trr, fs, fr,
 ):
     t = lax.axis_index("tok")
     e = lax.axis_index("exp")
@@ -121,16 +121,32 @@
     def token_part(a, block):
         return xg.at[a, rows(block), :]
 
-    def row_copy(a, i):
-        src = (xt, gt)[a]
-        return (
-            src, token_part(a, t), sx.at[2 * i + a], tr.at[2 * t + a],
-            y * SIDE + k + 2 * i, column_core,
-        )
-
-    def ring_copy(a, block, sem, tok):
-        part = token_part(a, block)
-        return remote(part, part, sem, tr.at[2 * block + a], tok, e)
+    def row_copy(i):
+        return (xt, token_part(0, t), sx.at[i], tr.at[2 * t], y * SIDE + k + 2 * i, column_core)
+
+    def ring_copy(block, sem, tok):
+        part = token_part(0, block)
+        return remote(part, part, sem, tr.at[2 * block], tok, e)
+
+    def row_at(dy):
+        return lax.rem(y + dy, ny)
+
+    def swing_copy(n):
+        return remote(gt, gstage.at[y], gs.at[n], gq.at[n], (above, below)[n], e)
+
+    def pass_copy(n):
+        part = gstage.at[row_at((ny - 1, 1)[n]), pl.ds(n * (rows_dev // 2), rows_dev // 2), :]
+        return remote(part, part, gs.at[2 + n], gq.at[2 + n], (above, below)[n], e)
+
+    def side_copy(dy, i):
+        row = row_at(dy)
+        block = row * SIDE + x
+        src = gt if dy == 0 else gstage.at[row]
+        return (src, token_part(1, block), gx.at[2 * dy + i], tr.at[2 * block + 1], y * SIDE + k + 2 * i, column_core)
+
+    def side(dy):
+        for i in range(2):
+            push(*side_copy(dy, i))
 
     def twin_copy(a, block, i):
         part = token_part(a, block)
@@ -157,8 +173,10 @@
 
     prob_copy = remote(p2.at[1 - k], pr, ps, prs, t, sibling)
     prob_copy.start()
-    for a in range(2):
-        loop(2, lambda i: push(*row_copy(a, i)))
+    for n in range(2):
+        swing_copy(n).start()
+    loop(2, lambda i: push(*row_copy(i)))
+    side(0)
 
     def send_line(s):
         loop(2 * ne, lambda i: push(*line_copy(s, i)))
@@ -167,22 +185,40 @@
     send_line(1)
 
     def forward_row(i):
-        for a in range(2):
-            block = row_block(0, i)
-            landed(token_part(a, block), tr.at[2 * block + a])
-            twin_copy(a, block, i).start()
-            ring_copy(a, block, sup.at[2 * i + a], above).start()
-            ring_copy(a, block, sdn.at[2 * i + a], below).start()
+        block = row_block(0, i)
+        landed(token_part(0, block), tr.at[2 * block])
+        twin_copy(0, block, i).start()
+        ring_copy(block, sup.at[i], above).start()
+        ring_copy(block, sdn.at[i], below).start()
 
     def forward_ring():
-        for a in range(2):
-            lower, upper = row_block(ny - 1, 0), row_block(1, 1)
-            landed(token_part(a, lower), tr.at[2 * lower + a])
-            ring_copy(a, lower, sup.at[4 + a], above).start()
-            twin_copy(a, lower, 2).start()
-            landed(token_part(a, upper), tr.at[2 * upper + a])
-            ring_copy(a, upper, sdn.at[4 + a], below).start()
-            twin_copy(a, upper, 3).start()
+        lower, upper = row_block(ny - 1, 0), row_block(1, 1)
+        landed(token_part(0, lower), tr.at[2 * lower])
+        ring_copy(lower, sup.at[2], above).start()
+        twin_copy(0, lower, 2).start()
+        landed(token_part(0, upper), tr.at[2 * upper])
+        ring_copy(upper, sdn.at[2], below).start()
+        twin_copy(0, upper, 3).start()
+
+    def forward_swing():
+        for n, dy in enumerate((ny - 1, 1)):
+            landed(gstage.at[row_at(dy)], gq.at[n])
+            pass_copy(n).start()
+            side(dy)
+
+    def forward_pass():
+        for n in range(2):
+            part = gstage.at[row_at(2), pl.ds(n * (rows_dev // 2), rows_dev // 2), :]
+            landed(part, gq.at[2 + n])
+        side(2)
+
+    def twin_row(dy):
+        def step(w):
+            block = row_block(dy, w)
+            landed(token_part(1, block), tr.at[2 * block + 1])
+            twin_copy(1, block, 2 * dy + w).start()
+
+        loop(2, step)
 
     def forward_weights(s):
         def step(i):
@@ -192,18 +228,21 @@
 
         loop(nt, step)
 
+    forward_swing()
     loop(2, forward_row)
     forward_weights(0)
+    forward_pass()
     send_line(2)
+    twin_row(0)
     forward_ring()
     forward_weights(1)
+    for dy in range(1, ny):
+        twin_row(dy)
     late = ((ny - 1, 1), (1, 0), (2, 0), (2, 1))
     for n, (dy, w) in enumerate(late):
-        for a in range(2):
-            block = row_block(dy, w)
-            landed(token_part(a, block), tr.at[2 * block + a])
-            twin_copy(a, block, 4 + n).start()
-
+        block = row_block(dy, w)
+        landed(token_part(0, block), tr.at[2 * block])
+        twin_copy(0, block, 4 + n).start()
     forward_weights(2)
 
     def take_tokens(i):
@@ -273,20 +312,21 @@
 
         loop(count, step, first)
 
-    def row_at(dy):
-        return lax.rem(y + dy, ny)
-
     def token_part_grads(part):
         weights = jnp.concatenate([ww[s, 0, part, :] for s in range(PARTS)], axis=1)
         return jnp.dot(weights, pa[...], preferred_element_type=F32)
 
     def pair_copy(n, dy):
         row = row_at(dy)
-        return remote(xg.at[0, pair_rows(row, 1 - k), :], cbuf.at[row], cs.at[n], cr.at[row], t, sibling)
+        src = spare.at[0] if n == 0 else xg.at[0, pair_rows(row, 1 - k), :]
+        return remote(src, cbuf.at[row], cs.at[n], cr.at[row], t, sibling)
 
     def give(n, dy):
         part = pair_rows(row_at(dy), 1 - k)
-        xg[0, part, :] = token_part_grads(part).astype(BF16)
+        if n == 0:
+            spare[0] = token_part_grads(part).astype(BF16)
+        else:
+            xg[0, part, :] = token_part_grads(part).astype(BF16)
         pair_copy(n, dy).start()
 
     def half_rows(row, w):
@@ -301,14 +341,14 @@
             total = total + cbuf[row, w * rows_dev:(w + 1) * rows_dev, :].astype(F32)
             for term in added[w]:
                 total = total + term[...].astype(F32)
-            xg[0, part, :] = total.astype(BF16)
-
-    def far_copies():
-        row = row_at(2)
-        return (
-            remote(xg.at[0, half_rows(row, 0), :], ring1.at[1], qs.at[0], qr.at[1], below, e),
-            remote(xg.at[0, half_rows(row, 1), :], ring1.at[0], qs.at[1], qr.at[0], above, e),
-        )
+            if dy == 2:
+                spare[1, w * rows_dev:(w + 1) * rows_dev, :] = total.astype(BF16)
+            else:
+                xg[0, part, :] = total.astype(BF16)
+
+    def far_copy(w):
+        src = spare.at[1, pl.ds(w * rows_dev, rows_dev), :]
+        return remote(src, ring1.at[1 - w], qs.at[w], qr.at[1 - w], (below, above)[w], e)
 
     def near_copy(n):
         src = xg.at[0, pair_rows(row_at((1, ny - 1)[n]), k), :]
@@ -323,23 +363,25 @@
     gives = (2, 1, ny - 1, 0)
     quarter = nt // 4
     last = PARTS - 1
-    for s in range(PARTS):
+    for s in range(last):
         hidden(s)
         weight_grads(s)
-        if s == last:
-            break
+    hidden(last)
+    give(0, 2)
+    keep(2, ((), ()))
+    for w in range(2):
+        far_copy(w).start()
+    weight_grads(last)
     forward_grads(0)
     loop(nt, lambda i: push(*gate_copy(i)))
+    for i in range(3):
+        ring_copy(t, sup.at[i], above).wait_send()
+        ring_copy(t, sdn.at[i], below).wait_send()
     for a in range(2):
-        for i in range(3):
-            ring_copy(a, t, sup.at[2 * i + a], above).wait_send()
-            ring_copy(a, t, sdn.at[2 * i + a], below).wait_send()
         loop(nt // 2, lambda i: twin_copy(a, t, i).wait_send())
     for n, dy in enumerate(gives):
-        give(n, dy)
-    keep(2, ((), ()))
-    for copy in far_copies():
-        copy.start()
+        if n > 0:
+            give(n, dy)
     forward_grads(last - 1)
     landed(ring1.at[0], qr.at[0])
     keep(1, ((), (ring1.at[0],)))
@@ -362,8 +404,13 @@
     loop(2, lambda i: landed(trecv.at[i], trr.at[i]))
     loop(nt, lambda i: landed(gpart.at[i], gr.at[i]))
     loop(nt, lambda i: sent(*gate_copy(i)))
-    for a in range(2):
-        loop(2, lambda i: sent(*row_copy(a, i)))
+    loop(2, lambda i: sent(*row_copy(i)))
+    for n in range(2):
+        swing_copy(n).wait_send()
+        pass_copy(n).wait_send()
+    for dy in range(ny):
+        for i in range(2):
+            sent(*side_copy(dy, i))
     for s in range(PARTS):
         loop(2 * ne, lambda i: sent(*line_copy(s, i)))
         loop(nt, lambda i: sent(*plane_copy(s, i)))
@@ -371,8 +418,9 @@
         loop(nt, lambda i: sent(*owner_copy(s, i)))
     for n, dy in enumerate(gives):
         pair_copy(n, dy).wait_send()
-    for copy in (*far_copies(), near_copy(0), near_copy(1)):
-        copy.wait_send()
+    for n in range(2):
+        far_copy(n).wait_send()
+        near_copy(n).wait_send()
     for w in range(2):
         sent(*row_owner(w))
 
@@ -387,7 +435,7 @@
     dma = pltpu.SemaphoreType.DMA
     anywhere = pl.BlockSpec(memory_space=pl.ANY)
     relay = jax.ShapeDtypeStruct(sw.shape, BF16)
-    counts = (6 * ne, 6 * ne, 4, 2 * nt, 6, 6, nt, 3 * nt, 3 * nt)
+    counts = (6 * ne, 6 * ne, 2, 2 * nt, 3, 3, nt, 4, 4, 2 * ny, 3 * nt, 3 * nt)
     counts_back = (3 * nt, 6 * ne, nt, nt, ny, ny, 4, 4, 2, 2, 3 * nt, 6 * ne)
     return pl.pallas_call(
         functools.partial(layer_kernel, nt, ne, rows_dev, hid, cols, htile, ntile),
@@ -397,9 +445,10 @@
             relay,
             jax.ShapeDtypeStruct((2, rows_dev, cols), BF16),
             jax.ShapeDtypeStruct((nt, 1, cols), F32),
+            jax.ShapeDtypeStruct((ny, rows_dev, cols), BF16),
         ),
         in_specs=[anywhere] * 3 + [pl.BlockSpec(memory_space=pltpu.VMEM)],
-        out_specs=(anywhere,) * 5,
+        out_specs=(anywhere,) * 6,
         scratch_shapes=[
             pltpu.VMEM((2, width, cols), BF16),
             pltpu.VMEM((PARTS, 2, width, htile), BF16),
@@ -408,6 +457,7 @@
             pltpu.VMEM((PARTS, 2, width, htile), BF16),
             pltpu.VMEM((ny, 2 * rows_dev, cols), BF16),
             pltpu.VMEM((2, rows_dev, cols), BF16),
+            pltpu.VMEM((2, 2 * rows_dev, cols), BF16),
             pltpu.VMEM((2, 2 * rows_dev, cols), BF16),
             pltpu.VMEM((2, htile, width), BF16),
             pltpu.VMEM((1, cols), F32),
@@ -490,7 +540,7 @@
     sw = take(ids, up_weight, down_weight)
     slots = 2 * (t // 2) + jnp.arange(2, dtype=jnp.int32)
     p2 = jnp.sum(jnp.where(routes[None] == slots[:, None, None], gate_probs[None], 0.0), axis=2)
-    _, _, wout, trecv, gpart = layer(sw, tokens.T, grad_out.T, p2[:, None, :], nt, ne)
+    _, _, wout, trecv, gpart, _ = layer(sw, tokens.T, grad_out.T, p2[:, None, :], nt, ne)
     token_grads = jnp.sum(trecv.astype(F32), axis=0).astype(BF16).T
     slot_ids = jnp.arange(nt, dtype=jnp.int32)
     hits = routes[None] == slot_ids[:, None, None]

time: 398 us -> 354 us (0.89); the launches traced: 390 us -> 352 us
  Pallas kernels: 379 us -> 341 us
    pallas_call x1, Pallas kernels: 361 us -> 323 us  [layer(): pl.pallas_call(functools.partial(layer_kernel, nt, ne, rows_dev, hid, col...]
where the time goes in v4:
time: 354 us; the launch traced here: 352 us
  Pallas kernels  341 us (96%)
  local copies, waits for them, and re-layouts  6.24 us (2%)
  other arithmetic  4.39 us (1%)
    pallas_call x1, Pallas kernels, layer(): pl.pallas_call(functools.partial(layer_kernel, nt, ne, rows_dev, hid, col...  323 us
    pallas_call x1, Pallas kernels, take(): pl.pallas_call(take_kernel, out_shape=jax.ShapeDtypeStruct((count, *block...  12.8 us

profile of v4, /device:TPU:0, one launch (start us, length us, event | category | flops | bytes accessed | tf_op | source)
XLA Modules:
  0.0 351.9 jit_solution(11585658692922409604)
XLA Ops:
  0.7 0.8 copy.21
  1.4 0.1 copy.22
  1.5 0.6 sub.16.ids
  2.1 1.0 fusion
  3.1 0.6 broadcast_in_dim.46.p2
  3.7 12.8 %shard_map.102.sw = bf16[16,3,2,160,256]{4,3,2,1,0:T(8,128)(2,1)} custom-call(s32[16]{0:T(128)} %sub.16.ids, bf16[10,160,768]{2,1,0:T(8,128)(2,1)} %up.1, bf16[10,160,768]{2,1,0:T(8,128)(2,1)} %down.1), custom_call_target="tpu_custom_call" | custom-call | tf_op jit(solution)/shard_map/pallas_call | solution.py:490
  16.6 0.0 copy-start.2
  16.6 0.0 copy-start.1
  16.6 322.6 %shard_map.103 = (bf16[16,3,2,160,256]{4,3,2,1,0:T(8,128)(2,1)}, bf16[16,3,2,160,256]{4,3,2,1,0:T(8,128)(2,1)}, bf16[16,3,2,160,256]{4,3,2,1,0:T(8,128)(2,1)}, b...) custom-call(bf16[16,3,2,160,256]{4,3,2,1,0:T(8,128)(2,1)} %shard_map.102.sw, ...), custom_call_target="tpu_custom_call" | custom-call | flops 40265318400 | bytes 67108864 | tf_op jit(solution)/shard_map/pallas_call | solution.py:440
  339.1 2.6 reduce_sum.31
  341.7 0.9 copy.25
  342.7 0.0 copy-done.2
  342.7 0.8 select_reduce_fusion
  343.5 0.0 copy-done.1
  343.5 0.0 copy-start
  343.5 3.2 copy-done
  346.7 5.2 %shard_map.104 = (bf16[10,160,768]{2,1,0:T(8,128)(2,1)}, bf16[10,160,768]{2,1,0:T(8,128)(2,1)}) custom-call(s32[16]{0:T(128)S(1)} %copy-done.1, bf16[16,3,2,160,256]{4,3,2,1,0:T(8,128)(2,1)S(1)} %copy-done), custom_call_target="tpu_custom_call" | custom-call | tf_op jit(solution)/shard_map/pallas_call | solution.py:520
  (2 shorter events, 0.0 us)
Async XLA Ops:
  16.6 326.1 %copy-start.2 = (s32[2048,6]{0,1:T(8,128)S(1)}, s32[2048,6]{0,1:T(8,128)}, u32[]{:S(2)}) copy-start(s32[2048,6]{0,1:T(8,128)} %param.10) | copy-start | bytes 147460
  16.6 326.9 %copy-start.1 = (s32[16]{0:T(128)S(1)}, s32[16]{0:T(128)}, u32[]{:S(2)}) copy-start(s32[16]{0:T(128)} %sub.16.ids) | copy-start | bytes 196
  343.5 3.2 copy-start
